TPU v7x, 32 devices: a whole 2x2x4 slice. The times are simulated.
32 devices in a mesh: wide: 8 (over z, y), rep: 4 (over x, core).
Axes of the slice: x: 2, y: 2, z: 4, core: 2. Of those that a mesh axis runs over, the one named last changes fastest.
Arguments:
- node_feats: bfloat16 [8192, 512], P('wide'), may hold values from -6 to 6
- w_self: bfloat16 [512, 512], replicated, may hold values from -0.25 to 0.25
- w_neigh: bfloat16 [512, 512], replicated, may hold values from -0.25 to 0.25
- send_rows: int32 [8, 8, 32], P('wide', None, 'rep'), may hold values from 0 to 1023
- tile_dst: int32 [8, 4, 128], P('wide', 'rep'), may hold values from 0 to 15
- tile_src: int32 [8, 4, 128], P('wide', 'rep'), may hold values from 0 to 16
- tile_bits: int32 [8, 4, 32768], P('wide', 'rep'), may hold values from 0 to 65280
- norm_count: int32 [8192], P('wide'), may hold values from 512 to 2048
- grad_out: bfloat16 [8192, 512], P(('wide', 'rep')), may hold values from -6 to 6
Outputs:
- out_feats: bfloat16 [8192, 512], P(('wide', 'rep'))
- grad_feats: bfloat16 [8192, 512], P(('wide', 'rep'))
- grad_self: bfloat16 [512, 512], replicated
- grad_neigh: bfloat16 [512, 512], replicated
All inputs are finite; a program needn't handle non-finite values.
Results may differ from a plain program's by a relative error of at most 0.014.
Values may be sent and summed in bfloat16 or wider, within the bound.
A program may use at most 64 MiB of HBM per device.

v0:
```python
import math

import jax
import jax.numpy as jnp
from jax import lax
from jax.sharding import PartitionSpec as P

BLOCK = 64


def unpack_bits(packed, tile_count, block_size):
    shaped = packed.reshape(tile_count, block_size, block_size // 16)
    shift_list = jnp.arange(16, dtype=jnp.int32)
    bit_grid = jnp.bitwise_and(jnp.right_shift(shaped[..., None], shift_list), 1)
    return bit_grid.reshape(tile_count, block_size, block_size)


def times_transposed(left, right):
    return lax.dot_general(
        left, right, (((1,), (1,)), ((), ())), preferred_element_type=jnp.float32
    )


def on_device(
    node_feats, w_self, w_neigh, send_rows, tile_dst, tile_src, tile_bits, norm_count, grad_out
):
    node_rows, feat_width = node_feats.shape
    peer_count = lax.axis_size("wide")
    replicas = lax.axis_size("rep")
    slot_count = send_rows.shape[2]
    tile_total = tile_dst.shape[2]
    block_size = BLOCK
    quarter = node_rows // replicas
    rep_index = lax.axis_index("rep")
    dst_count = node_rows // block_size
    group_size = math.gcd(tile_total, 32)
    send_index = send_rows[0]
    outgoing = jnp.take(node_feats, send_index.reshape(-1), axis=0).reshape(
        peer_count, slot_count, feat_width
    )
    incoming = lax.all_to_all(outgoing, "wide", split_axis=0, concat_axis=0, tiled=True)
    src_table = jnp.concatenate(
        [node_feats, incoming.reshape(peer_count * slot_count, feat_width)], axis=0
    )
    source_blocks = src_table.reshape(-1, block_size, feat_width)
    src_count = source_blocks.shape[0]
    tile_masks = unpack_bits(tile_bits[0, 0], tile_total, block_size).astype(jnp.bfloat16)
    grouped_masks = tile_masks.reshape(-1, group_size, block_size, block_size)
    grouped_dst = tile_dst[0, 0].reshape(-1, group_size)
    grouped_src = tile_src[0, 0].reshape(-1, group_size)

    def forward_group(running, group_items):
        mask_part, dst_part, src_part = group_items
        picked = jnp.take(source_blocks, src_part, axis=0)
        products = jnp.einsum("tij,tjf->tif", mask_part, picked, preferred_element_type=jnp.float32)
        return (running.at[dst_part].add(products), None)

    partial_sum, _ = lax.scan(
        forward_group,
        jnp.zeros((dst_count, block_size, feat_width), jnp.float32),
        (grouped_masks, grouped_dst, grouped_src),
    )
    partial_sum = partial_sum.reshape(node_rows, feat_width)
    summed = lax.psum(partial_sum, "rep")
    own_sums = lax.dynamic_slice_in_dim(summed, rep_index * quarter, quarter, 0)
    scale_all = lax.rsqrt(norm_count.astype(jnp.float32))
    own_scale = lax.dynamic_slice_in_dim(scale_all, rep_index * quarter, quarter, 0)
    own_feats = lax.dynamic_slice_in_dim(node_feats, rep_index * quarter, quarter, 0)
    own_agg = (own_sums * own_scale[:, None]).astype(jnp.bfloat16)
    pre_act = jnp.dot(own_feats, w_self, preferred_element_type=jnp.float32) + jnp.dot(
        own_agg, w_neigh, preferred_element_type=jnp.float32
    )
    sigmoid = jax.nn.sigmoid(pre_act)
    out_feats = (pre_act * sigmoid).astype(jnp.bfloat16)
    grad_pre = (grad_out.astype(jnp.float32) * sigmoid * (1.0 + pre_act * (1.0 - sigmoid))).astype(
        jnp.bfloat16
    )
    dims_rows = (((0,), (0,)), ((), ()))
    self_term = lax.dot_general(own_feats, grad_pre, dims_rows, preferred_element_type=jnp.float32)
    neigh_term = lax.dot_general(own_agg, grad_pre, dims_rows, preferred_element_type=jnp.float32)
    summed_self, summed_neigh = lax.psum((self_term, neigh_term), ("wide", "rep"))
    own_grad_agg = (times_transposed(grad_pre, w_neigh) * own_scale[:, None]).astype(jnp.bfloat16)
    grad_agg = lax.all_gather(own_grad_agg, "rep", axis=0, tiled=True)
    agg_blocks = grad_agg.reshape(dst_count, block_size, feat_width)

    def backward_group(running, group_items):
        mask_part, dst_part, src_part = group_items
        picked = jnp.take(agg_blocks, dst_part, axis=0)
        products = jnp.einsum("tij,tif->tjf", mask_part, picked, preferred_element_type=jnp.float32)
        return (running.at[src_part].add(products), None)

    table_grad, _ = lax.scan(
        backward_group,
        jnp.zeros((src_count, block_size, feat_width), jnp.float32),
        (grouped_masks, grouped_dst, grouped_src),
    )
    table_grad = table_grad.reshape(src_count * block_size, feat_width)
    local_grad = table_grad[:node_rows]
    halo_grad = (
        table_grad[node_rows:].astype(jnp.bfloat16).reshape(peer_count, slot_count, feat_width)
    )
    returned = lax.all_to_all(halo_grad, "wide", split_axis=0, concat_axis=0, tiled=True)
    returned_rows = (
        jnp.zeros((node_rows, feat_width), jnp.float32)
        .at[send_index.reshape(-1)]
        .add(returned.reshape(-1, feat_width).astype(jnp.float32))
    )
    own_total = lax.psum_scatter(
        (local_grad + returned_rows).astype(jnp.bfloat16), "rep", scatter_dimension=0, tiled=True
    ).astype(jnp.float32)
    grad_feats = (own_total + times_transposed(grad_pre, w_self)).astype(jnp.bfloat16)
    return (
        out_feats,
        grad_feats,
        summed_self.astype(jnp.bfloat16),
        summed_neigh.astype(jnp.bfloat16),
    )


def solution(mesh):
    in_specs = (
        P("wide", None),
        P(),
        P(),
        P("wide", None, "rep"),
        P("wide", "rep", None),
        P("wide", "rep", None),
        P("wide", "rep", None),
        P("wide"),
        P(("wide", "rep"), None),
    )
    out_specs = (P(("wide", "rep"), None), P(("wide", "rep"), None), P(), P())
    return jax.shard_map(
        on_device, mesh=mesh, in_specs=in_specs, out_specs=out_specs, check_vma=False
    )
```

profile of v0, /device:TPU:0, one launch (start us, length us, event | category | flops | bytes accessed | tf_op | source)
XLA Modules:
  0.0 322.5 jit_solution(16487835407087848897)
XLA Ops:
  12.1 7.3 %all-to-all-start = ((bf16[8,8,512]{2,1,0:T(8,128)(2,1)}), bf16[8,8,512]{2,1,0:T(8,128)(2,1)S(1)}, u32[]{:S(2)}, u32[]{:S(2)}) async-start(bf16[8,8,512]{2,1,0:T(8,128)(2,1)} %bitcast_select_fusion), calls=%async_computation | async-start | bytes 131072 | tf_op jit(solution)/shard_map/all_to_all | solution.py:41
  21.9 5.7 %shift_right_arithmetic.23 = s32[128,64,4]{2,1,0:T(8,128)} reshape(s32[32768]{0:T(1024)S(1)} %reduce.10) | data formatting | bytes 262144 | tf_op jit(solution)/shard_map/shift_right_arithmetic | solution.py:14
  35.9 57.0 %while.20 = (s32[]{:T(128)}, f32[16,64,512]{2,1,0:T(8,128)S(1)}, s32[4,32]{1,0:T(4,128)S(1)}, bf16[4,32,64,64]{2,3,1,0:T(8,128)(2,1)}, s32[4,32]{1,0:T(4,128)S(1)}, /*index=5*/bf16[17,64,512]{2,1,0:T(8,128)(2,1)}, s32[]{:T(128)}) while((s32[]{:T(128)}, f32[16,64,512]{2,1,0:T(8,128)S(1)}, s32[4,32]{1,0:T(4,128)S(1)}, ...), condition=%wide.region_2.3_spmd, body=%wide.region_0.0_spmd.sunk | while | flops 136316288 | bytes 23598240 | solution.py:58
  36.0 3.2 %gather_fusion = bf16[32,64,512]{2,1,0:T(8,128)(2,1)} fusion(bf16[17,64,512]{2,1,0:T(8,128)(2,1)} %get-tuple-element.215, s32[1024]{0:T(1024)S(1)} %pad_clamp_fusion.5), kind=kCustom, calls=%fused_computation.clone.1 | custom fusion | bytes 4194432 | tf_op jit(solution)/shard_map/while/body/eval_jaxpr/jit(_take)/gather | solution.py:54
  39.2 4.5 %fusion.55 = f32[32,64,512]{2,1,0:T(8,128)} fusion(bf16[32,64,512]{2,1,0:T(8,128)(2,1)} %gather_fusion, pred[32]{0:T(512)(128)(4,1)S(1)} %compare_and_fusion.5, bf16[4,32,64,64]{2,3,1,0:T(8,128)(2,1)} %get-tuple-element.213, s32[]{:T(128)S(6)} %copy.22), kind=kOutput, calls=%fused_computation.6.clone.1 | convolution fusion | flops 135266304 | bytes 6815780 | tf_op jit(solution)/shard_map/while/body/eval_jaxpr/tij,tjf->tif/dot_general | solution.py:55
  43.7 6.5 %scatter_fusion = f32[16,64,512]{2,1,0:T(8,128)S(1)} fusion(f32[16,64,512]{2,1,0:T(8,128)S(1)} %get-tuple-element.204, s32[32]{0:T(128)S(1)} %get-tuple-element.186, f32[32,64,512]{2,1,0:T(8,128)} %fusion.55), kind=kCustom, calls=%fused_computation.3.clone.1 | custom fusion | flops 1048576 | bytes 12583040 | tf_op jit(solution)/shard_map/while/body/eval_jaxpr/scatter-add | solution.py:56
  50.3 3.2 %gather_fusion = bf16[32,64,512]{2,1,0:T(8,128)(2,1)} fusion(bf16[17,64,512]{2,1,0:T(8,128)(2,1)} %get-tuple-element.215, s32[1024]{0:T(1024)S(1)} %pad_clamp_fusion.5), kind=kCustom, calls=%fused_computation.clone.1 | custom fusion | bytes 4194432 | tf_op jit(solution)/shard_map/while/body/eval_jaxpr/jit(_take)/gather | solution.py:54
  53.5 4.5 %fusion.55 = f32[32,64,512]{2,1,0:T(8,128)} fusion(bf16[32,64,512]{2,1,0:T(8,128)(2,1)} %gather_fusion, pred[32]{0:T(512)(128)(4,1)S(1)} %compare_and_fusion.5, bf16[4,32,64,64]{2,3,1,0:T(8,128)(2,1)} %get-tuple-element.213, s32[]{:T(128)S(6)} %copy.22), kind=kOutput, calls=%fused_computation.6.clone.1 | convolution fusion | flops 135266304 | bytes 6815780 | tf_op jit(solution)/shard_map/while/body/eval_jaxpr/tij,tjf->tif/dot_general | solution.py:55
  58.0 6.5 %scatter_fusion = f32[16,64,512]{2,1,0:T(8,128)S(1)} fusion(f32[16,64,512]{2,1,0:T(8,128)S(1)} %get-tuple-element.204, s32[32]{0:T(128)S(1)} %get-tuple-element.186, f32[32,64,512]{2,1,0:T(8,128)} %fusion.55), kind=kCustom, calls=%fused_computation.3.clone.1 | custom fusion | flops 1048576 | bytes 12583040 | tf_op jit(solution)/shard_map/while/body/eval_jaxpr/scatter-add | solution.py:56
  67.8 4.5 %fusion.55 = f32[32,64,512]{2,1,0:T(8,128)} fusion(bf16[32,64,512]{2,1,0:T(8,128)(2,1)} %gather_fusion, pred[32]{0:T(512)(128)(4,1)S(1)} %compare_and_fusion.5, bf16[4,32,64,64]{2,3,1,0:T(8,128)(2,1)} %get-tuple-element.213, s32[]{:T(128)S(6)} %copy.22), kind=kOutput, calls=%fused_computation.6.clone.1 | convolution fusion | flops 135266304 | bytes 6815780 | tf_op jit(solution)/shard_map/while/body/eval_jaxpr/tij,tjf->tif/dot_general | solution.py:55
  72.2 6.5 %scatter_fusion = f32[16,64,512]{2,1,0:T(8,128)S(1)} fusion(f32[16,64,512]{2,1,0:T(8,128)S(1)} %get-tuple-element.204, s32[32]{0:T(128)S(1)} %get-tuple-element.186, f32[32,64,512]{2,1,0:T(8,128)} %fusion.55), kind=kCustom, calls=%fused_computation.3.clone.1 | custom fusion | flops 1048576 | bytes 12583040 | tf_op jit(solution)/shard_map/while/body/eval_jaxpr/scatter-add | solution.py:56
  82.0 4.5 %fusion.55 = f32[32,64,512]{2,1,0:T(8,128)} fusion(bf16[32,64,512]{2,1,0:T(8,128)(2,1)} %gather_fusion, pred[32]{0:T(512)(128)(4,1)S(1)} %compare_and_fusion.5, bf16[4,32,64,64]{2,3,1,0:T(8,128)(2,1)} %get-tuple-element.213, s32[]{:T(128)S(6)} %copy.22), kind=kOutput, calls=%fused_computation.6.clone.1 | convolution fusion | flops 135266304 | bytes 6815780 | tf_op jit(solution)/shard_map/while/body/eval_jaxpr/tij,tjf->tif/dot_general | solution.py:55
  86.5 6.5 %scatter_fusion = f32[16,64,512]{2,1,0:T(8,128)S(1)} fusion(f32[16,64,512]{2,1,0:T(8,128)S(1)} %get-tuple-element.204, s32[32]{0:T(128)S(1)} %get-tuple-element.186, f32[32,64,512]{2,1,0:T(8,128)} %fusion.55), kind=kCustom, calls=%fused_computation.3.clone.1 | custom fusion | flops 1048576 | bytes 12583040 | tf_op jit(solution)/shard_map/while/body/eval_jaxpr/scatter-add | solution.py:56
  95.8 51.5 %all-reduce.4.cloned.1.call-done = f32[1024,512]{1,0:T(8,128)} async-done(((f32[1024,512]{1,0:T(8,128)}), f32[1024,512]{1,0:T(8,128)}) %all-reduce.4.cloned.1.call-update) | async-done | bytes 2097168 | tf_op jit(solution)/shard_map/psum | solution.py:64
  150.7 17.0 %all-gather.2.cloned.1.call-done = bf16[1024,512]{1,0:T(8,128)(2,1)} async-done(((bf16[256,512]{1,0:T(8,128)(2,1)}), bf16[1024,512]{1,0:T(8,128)(2,1)}) %all-gather.2.cloned.1.call-update) | async-done | bytes 1048592 | tf_op jit(solution)/shard_map/all_gather | solution.py:83
  167.9 58.7 %while.21 = (s32[]{:T(128)}, f32[17,64,512]{2,1,0:T(8,128)S(1)}, s32[4,32]{1,0:T(4,128)S(1)}, bf16[4,32,64,64]{2,3,1,0:T(8,128)(2,1)}, s32[4,32]{1,0:T(4,128)S(1)}, /*index=5*/bf16[16,64,512]{2,1,0:T(8,128)(2,1)}, s32[]{:T(128)}) while((s32[]{:T(128)}, f32[17,64,512]{2,1,0:T(8,128)S(1)}, s32[4,32]{1,0:T(4,128)S(1)}, ...), condition=%wide.region_6.7_spmd, body=%wide.region_4.6_spmd.sunk | while | flops 136316288 | bytes 23598720 | solution.py:92
  168.5 3.3 %gather_fusion.1 = bf16[32,64,512]{2,1,0:T(8,128)(2,1)} fusion(bf16[16,64,512]{2,1,0:T(8,128)(2,1)} %get-tuple-element.236, s32[1024]{0:T(1024)S(1)} %pad_clamp_fusion.6), kind=kCustom, calls=%fused_computation.1.clone.1 | custom fusion | bytes 4194432 | tf_op jit(solution)/shard_map/while/body/eval_jaxpr/jit(_take)/gather | solution.py:88
  171.7 4.4 %fusion.59 = f32[32,64,512]{2,1,0:T(8,128)} fusion(bf16[32,64,512]{2,1,0:T(8,128)(2,1)} %gather_fusion.1, pred[32]{0:T(512)(128)(4,1)} %compare_and_fusion.6, bf16[4,32,64,64]{2,3,1,0:T(8,128)(2,1)} %get-tuple-element.234, s32[]{:T(128)S(6)} %copy.29), kind=kOutput, calls=%fused_computation.24.clone.1 | convolution fusion | flops 135266304 | bytes 6816260 | tf_op jit(solution)/shard_map/while/body/eval_jaxpr/tij,tif->tjf/dot_general | solution.py:89
  176.1 6.5 %scatter_fusion.1 = f32[17,64,512]{2,1,0:T(8,128)S(1)} fusion(f32[17,64,512]{2,1,0:T(8,128)S(1)} %get-tuple-element.225, s32[32]{0:T(128)S(1)} %get-tuple-element.194, f32[32,64,512]{2,1,0:T(8,128)} %fusion.59), kind=kCustom, calls=%fused_computation.4.clone.1 | custom fusion | flops 1048576 | bytes 12583040 | tf_op jit(solution)/shard_map/while/body/eval_jaxpr/scatter-add | solution.py:90
  183.2 3.3 %gather_fusion.1 = bf16[32,64,512]{2,1,0:T(8,128)(2,1)} fusion(bf16[16,64,512]{2,1,0:T(8,128)(2,1)} %get-tuple-element.236, s32[1024]{0:T(1024)S(1)} %pad_clamp_fusion.6), kind=kCustom, calls=%fused_computation.1.clone.1 | custom fusion | bytes 4194432 | tf_op jit(solution)/shard_map/while/body/eval_jaxpr/jit(_take)/gather | solution.py:88
  186.4 4.4 %fusion.59 = f32[32,64,512]{2,1,0:T(8,128)} fusion(bf16[32,64,512]{2,1,0:T(8,128)(2,1)} %gather_fusion.1, pred[32]{0:T(512)(128)(4,1)} %compare_and_fusion.6, bf16[4,32,64,64]{2,3,1,0:T(8,128)(2,1)} %get-tuple-element.234, s32[]{:T(128)S(6)} %copy.29), kind=kOutput, calls=%fused_computation.24.clone.1 | convolution fusion | flops 135266304 | bytes 6816260 | tf_op jit(solution)/shard_map/while/body/eval_jaxpr/tij,tif->tjf/dot_general | solution.py:89
  190.8 6.5 %scatter_fusion.1 = f32[17,64,512]{2,1,0:T(8,128)S(1)} fusion(f32[17,64,512]{2,1,0:T(8,128)S(1)} %get-tuple-element.225, s32[32]{0:T(128)S(1)} %get-tuple-element.194, f32[32,64,512]{2,1,0:T(8,128)} %fusion.59), kind=kCustom, calls=%fused_computation.4.clone.1 | custom fusion | flops 1048576 | bytes 12583040 | tf_op jit(solution)/shard_map/while/body/eval_jaxpr/scatter-add | solution.py:90
  197.8 3.3 %gather_fusion.1 = bf16[32,64,512]{2,1,0:T(8,128)(2,1)} fusion(bf16[16,64,512]{2,1,0:T(8,128)(2,1)} %get-tuple-element.236, s32[1024]{0:T(1024)S(1)} %pad_clamp_fusion.6), kind=kCustom, calls=%fused_computation.1.clone.1 | custom fusion | bytes 4194432 | tf_op jit(solution)/shard_map/while/body/eval_jaxpr/jit(_take)/gather | solution.py:88
  201.1 4.4 %fusion.59 = f32[32,64,512]{2,1,0:T(8,128)} fusion(bf16[32,64,512]{2,1,0:T(8,128)(2,1)} %gather_fusion.1, pred[32]{0:T(512)(128)(4,1)} %compare_and_fusion.6, bf16[4,32,64,64]{2,3,1,0:T(8,128)(2,1)} %get-tuple-element.234, s32[]{:T(128)S(6)} %copy.29), kind=kOutput, calls=%fused_computation.24.clone.1 | convolution fusion | flops 135266304 | bytes 6816260 | tf_op jit(solution)/shard_map/while/body/eval_jaxpr/tij,tif->tjf/dot_general | solution.py:89
  205.5 6.5 %scatter_fusion.1 = f32[17,64,512]{2,1,0:T(8,128)S(1)} fusion(f32[17,64,512]{2,1,0:T(8,128)S(1)} %get-tuple-element.225, s32[32]{0:T(128)S(1)} %get-tuple-element.194, f32[32,64,512]{2,1,0:T(8,128)} %fusion.59), kind=kCustom, calls=%fused_computation.4.clone.1 | custom fusion | flops 1048576 | bytes 12583040 | tf_op jit(solution)/shard_map/while/body/eval_jaxpr/scatter-add | solution.py:90
  212.5 3.3 %gather_fusion.1 = bf16[32,64,512]{2,1,0:T(8,128)(2,1)} fusion(bf16[16,64,512]{2,1,0:T(8,128)(2,1)} %get-tuple-element.236, s32[1024]{0:T(1024)S(1)} %pad_clamp_fusion.6), kind=kCustom, calls=%fused_computation.1.clone.1 | custom fusion | bytes 4194432 | tf_op jit(solution)/shard_map/while/body/eval_jaxpr/jit(_take)/gather | solution.py:88
  215.8 4.4 %fusion.59 = f32[32,64,512]{2,1,0:T(8,128)} fusion(bf16[32,64,512]{2,1,0:T(8,128)(2,1)} %gather_fusion.1, pred[32]{0:T(512)(128)(4,1)} %compare_and_fusion.6, bf16[4,32,64,64]{2,3,1,0:T(8,128)(2,1)} %get-tuple-element.234, s32[]{:T(128)S(6)} %copy.29), kind=kOutput, calls=%fused_computation.24.clone.1 | convolution fusion | flops 135266304 | bytes 6816260 | tf_op jit(solution)/shard_map/while/body/eval_jaxpr/tij,tif->tjf/dot_general | solution.py:89
  220.2 6.5 %scatter_fusion.1 = f32[17,64,512]{2,1,0:T(8,128)S(1)} fusion(f32[17,64,512]{2,1,0:T(8,128)S(1)} %get-tuple-element.225, s32[32]{0:T(128)S(1)} %get-tuple-element.194, f32[32,64,512]{2,1,0:T(8,128)} %fusion.59), kind=kCustom, calls=%fused_computation.4.clone.1 | custom fusion | flops 1048576 | bytes 12583040 | tf_op jit(solution)/shard_map/while/body/eval_jaxpr/scatter-add | solution.py:90
  227.3 5.6 %all-to-all-start.1 = ((bf16[8,8,512]{2,1,0:T(8,128)(2,1)}), bf16[8,8,512]{2,1,0:T(8,128)(2,1)}, u32[]{:S(2)}, u32[]{:S(2)}) async-start(bf16[8,8,512]{2,1,0:T(8,128)(2,1)} %fusion.30), calls=%async_computation.1 | async-start | bytes 131072 | tf_op jit(solution)/shard_map/all_to_all | solution.py:102
  234.5 5.4 %all-to-all-done.1 = bf16[8,8,512]{2,1,0:T(8,128)(2,1)} async-done(((bf16[8,8,512]{2,1,0:T(8,128)(2,1)}), bf16[8,8,512]{2,1,0:T(8,128)(2,1)}, u32[]{:S(2)}, u32[]{:S(2)}) %all-to-all-start.1) | async-done | bytes 65568 | tf_op jit(solution)/shard_map/all_to_all | solution.py:102
  239.9 4.2 %scatter_custom_fusion.2 = f32[1024,512]{1,0:T(8,128)} fusion(f32[1024,512]{1,0:T(8,128)} %bitcast.85, s32[64]{0:T(128)} %copy-done.7, bf16[8,8,512]{2,1,0:T(8,128)(2,1)} %all-to-all-done.1), kind=kCustom, calls=%fused_computation.58 | custom fusion | flops 65536 | bytes 2162688 | tf_op jit(solution)/shard_map/scatter-add | solution.py:106
  249.6 64.5 %all-reduce.5 = (bf16[512,512]{1,0:T(8,128)(2,1)}, bf16[512,512]{1,0:T(8,128)(2,1)}) all-reduce(f32[512,512]{1,0:T(8,128)S(1)} %fusion.24, f32[512,512]{1,0:T(8,128)S(1)} %fusion.35), channel_id=1, replica_groups=mesh['wide'=8,'rep'=4] {'wide','rep'}, use_global_device_ids=true, to_apply=%region_9.10 | all-reduce | flops 524288 | bytes 3145728 | tf_op jit(solution)/shard_map/psum | solution.py:81
  (85 shorter events, 40.6 us)
Async XLA Ops:
  7.2 140.1 %copy-start = (bf16[512,512]{1,0:T(8,128)(2,1)S(1)}, bf16[512,512]{1,0:T(8,128)(2,1)}, u32[]{:S(2)}) copy-start(bf16[512,512]{1,0:T(8,128)(2,1)} %param.15) | copy-start | bytes 1572868
  8.7 0.6 copy-start.7
  12.1 22.5 %all-to-all-start = ((bf16[8,8,512]{2,1,0:T(8,128)(2,1)}), bf16[8,8,512]{2,1,0:T(8,128)(2,1)S(1)}, u32[]{:S(2)}, u32[]{:S(2)}) async-start(bf16[8,8,512]{2,1,0:T(8,128)(2,1)} %bitcast_select_fusion), calls=%async_computation | async-start | bytes 131072 | tf_op jit(solution)/shard_map/all_to_all | solution.py:41
  19.4 127.9 %all-reduce.4.cloned.1.call-start = ((), (), s32[]{:S(2)}) async-start(), calls=%async_computation.3 | async-start | bytes 4194304 | tf_op jit(solution)/shard_map/psum | solution.py:64
  30.9 2.2 copy-start.8
  30.9 2.8 copy-start.9
  30.9 3.6 %copy-start.2 = (bf16[1024,512]{1,0:T(8,128)(2,1)S(1)}, bf16[1024,512]{1,0:T(8,128)(2,1)}, u32[]{:S(2)}) copy-start(bf16[1024,512]{1,0:T(8,128)(2,1)} %param.13) | copy-start | bytes 3145732
  93.0 1.3 copy-start.1
  93.0 1.4 copy-start.6
  93.0 1.5 copy-start.3
  94.3 73.3 %all-gather.2.cloned.1.call-start = ((), (), s32[]{:S(2)}) async-start(), calls=%async_computation.4 | async-start | bytes 1310720 | tf_op jit(solution)/shard_map/all_gather | solution.py:83
  94.5 55.1 %copy-start.4 = (f32[256]{0:T(256)}, f32[256]{0:T(256)S(1)}, u32[]{:S(2)}) copy-start(f32[256]{0:T(256)S(1)} %dynamic_slice.31) | copy-start | bytes 3076
  227.3 12.6 %all-to-all-start.1 = ((bf16[8,8,512]{2,1,0:T(8,128)(2,1)}), bf16[8,8,512]{2,1,0:T(8,128)(2,1)}, u32[]{:S(2)}, u32[]{:S(2)}) async-start(bf16[8,8,512]{2,1,0:T(8,128)(2,1)} %fusion.30), calls=%async_computation.1 | async-start | bytes 131072 | tf_op jit(solution)/shard_map/all_to_all | solution.py:102
  232.9 81.1 %reduce-scatter.2.cloned.1.call-start = ((), (), s32[]{:S(2)}) async-start(), calls=%async_computation.5 | async-start | bytes 1310720 | tf_op jit(solution)/shard_map/reduce_scatter | solution.py:108
  244.0 2.8 copy-start.5
Sparse Core Ops, SparseCore 0:
  94.5 52.7 all-reduce.3
  150.8 16.7 all-gather.1
  246.9 23.8 reduce-scatter.1
where the time goes:
time: 324 us; the launch traced here: 323 us
  waiting for transfers between devices  73.9 us (23%)
  other arithmetic  68.9 us (21%)
  blocking collectives  64.5 us (20%)
  matrix products  44.6 us (14%)
  local copies, waits for them, and re-layouts  43.5 us (13%)
  between operations  13.9 us (4%)
  starting transfers between devices  13 us (4%)
    psum x1, blocking collectives, on_device(): lax.psum((self_term, neigh_term), ('wide', 'rep'))  64.5 us
    psum x1, waiting for transfers between devices, on_device(): summed = lax.psum(partial_sum, 'rep')  51.5 us
    scatter-add x4, other arithmetic, forward_group(): return (running.at[dst_part].add(products), None)  25.9 us
    scatter-add x4, other arithmetic, backward_group(): return (running.at[src_part].add(products), None)  25.9 us
    dot_general x4, matrix products, forward_group(): jnp.einsum('tij,tjf->tif', mask_part, picked, preferred_element_type=jnp....  17.8 us
    dot_general x4, matrix products, backward_group(): jnp.einsum('tij,tif->tjf', mask_part, picked, preferred_element_type=jnp....  17.5 us
    all_gather x1, waiting for transfers between devices, on_device(): grad_agg = lax.all_gather(own_grad_agg, 'rep', axis=0, tiled=True)  17 us
    gather x4, local copies, waits for them, and re-layouts, backward_group(): picked = jnp.take(agg_blocks, dst_part, axis=0)  13.1 us
  transfers between devices with their start and end apart: 5, of which 3 were waited for; matrix products, arithmetic and copies ran while one was open for 6% of the time, Pallas kernels for 0%

commit v1 on v0

v1 whole, which is shorter than its diff:
```python
import functools

import jax
import jax.numpy as jnp
from jax import lax
from jax.experimental import pallas as pl
from jax.experimental.pallas import tpu as pltpu
from jax.sharding import PartitionSpec as P

BLOCK = 64
GROUP = 32
LANES = 128
MESH = pl.DeviceIdType.MESH
VMEM_BYTES = 56 * 1024 * 1024


def partners(replicas):
    mine = lax.axis_index("rep")
    core = mine + 1 - 2 * lax.rem(mine, 2)
    across = lax.rem(mine + 2, replicas)
    diagonal = lax.rem(core + 2, replicas)
    return mine, core, across, diagonal


def enter(peer_count, mine_wide, mine, core, across):
    barrier = pltpu.get_barrier_semaphore()
    for step in range(1, peer_count):
        peer = lax.rem(mine_wide + step, peer_count)
        pl.semaphore_signal(barrier, inc=1, device_id=(peer, mine), device_id_type=MESH)
    for other in (core, across):
        pl.semaphore_signal(barrier, inc=1, device_id=(mine_wide, other), device_id_type=MESH)
    pl.semaphore_wait(barrier, peer_count + 1)


def times_transposed(left, right):
    return lax.dot_general(
        left, right, (((1,), (1,)), ((), ())), preferred_element_type=jnp.float32
    )


def transposed_times(left, right):
    return lax.dot_general(
        left, right, (((0,), (0,)), ((), ())), preferred_element_type=jnp.float32
    )


def spread_inputs(
    peer_count,
    slots,
    bits,
    meta,
    grad_out,
    index_col,
    feats,
    all_bits,
    all_meta,
    all_grad,
    all_halo,
    outgoing,
    local_sem,
    send_sem,
    recv_sem,
    halo_send,
    halo_recv,
):
    mine_wide = lax.axis_index("wide")
    mine, core, across, diagonal = partners(4)
    enter(peer_count, mine_wide, mine, core, across)

    def push(src, dst, which, wide_to, rep_to):
        return pltpu.make_async_remote_copy(
            src_ref=src,
            dst_ref=dst,
            send_sem=send_sem.at[which],
            recv_sem=recv_sem.at[which],
            device_id=(wide_to, rep_to),
            device_id_type=MESH,
        )

    pairs = ((bits, all_bits), (meta, all_meta), (grad_out, all_grad))
    to_across = [
        push(src, dst.at[mine], n, mine_wide, across) for n, (src, dst) in enumerate(pairs)
    ]
    to_core = [
        push(src, dst.at[mine], 4 + n, mine_wide, core) for n, (src, dst) in enumerate(pairs)
    ]
    own = [
        pltpu.make_async_copy(src, dst.at[mine], local_sem.at[n])
        for n, (src, dst) in enumerate(pairs)
    ]
    for copy in to_across + to_core + own:
        copy.start()
    node_rows = feats.shape[0]
    half = feats.shape[1] // 2
    for first in range(0, peer_count * slots, 64):
        picks = index_col[first : first + 64, :]
        chosen = picks == lax.broadcasted_iota(jnp.int32, (64, node_rows), 1)
        rows = jnp.dot(
            chosen.astype(jnp.bfloat16), feats[...], preferred_element_type=jnp.float32
        )
        for n in range(64 // slots):
            part = rows[n * slots : (n + 1) * slots]
            outgoing[first // slots + n] = jnp.concatenate(
                [part[:, :half], part[:, half:]], axis=0
            ).astype(jnp.bfloat16)
    exchange = []
    for step in range(1, peer_count):
        peer = lax.rem(mine_wide + step, peer_count)
        copy = pltpu.make_async_remote_copy(
            src_ref=outgoing.at[peer],
            dst_ref=all_halo.at[mine, mine_wide],
            send_sem=halo_send.at[step],
            recv_sem=halo_recv.at[step],
            device_id=(peer, mine),
            device_id_type=MESH,
        )
        copy.start()
        exchange.append(copy)
    kept = pltpu.make_async_copy(
        outgoing.at[mine_wide], all_halo.at[mine, mine_wide], local_sem.at[3]
    )
    kept.start()
    kept.wait()
    for copy in exchange:
        copy.wait_recv()
    halo_across = push(all_halo.at[mine], all_halo.at[mine], 3, mine_wide, across)
    halo_core = push(all_halo.at[mine], all_halo.at[mine], 7, mine_wide, core)
    halo_across.start()
    halo_core.start()
    onward = []
    for n, (came, dst) in enumerate(
        zip(to_across + [halo_across], (all_bits, all_meta, all_grad, all_halo))
    ):
        came.wait_recv()
        copy = push(dst.at[across], dst.at[across], 8 + n, mine_wide, core)
        copy.start()
        onward.append(copy)
    for copy in to_core + [halo_core] + onward:
        copy.wait_recv()
    for copy in to_across + to_core + [halo_across, halo_core] + onward + exchange:
        copy.wait_send()
    for copy in own:
        copy.wait()


def layer(
    peer_count,
    slots,
    meta,
    bits,
    grad_out,
    halo,
    feats,
    w_self,
    w_neigh,
    norm,
    out_feats,
    own_grad,
    halo_grad,
    weight_grad,
    blocks,
    adjacency,
    table,
    lhs,
    scale,
    agg,
    grad_pre,
    grad_agg,
):
    replicas = bits.shape[0]
    mine = lax.axis_index("rep")
    node_rows, width = feats.shape
    half = width // 2
    dst_count = node_rows // BLOCK
    halo_rows = peer_count * slots
    halo_blocks = halo_rows // BLOCK
    pair_count = (dst_count + replicas * halo_blocks) // 2
    groups = bits.shape[1] // BLOCK
    quarter = node_rows // replicas

    blocks[...] = jnp.zeros_like(blocks)
    for r in range(replicas):
        words = bits[r]
        rows = pl.ds(r * words.shape[0], words.shape[0])
        lhs[rows, :LANES] = (words & 255).astype(jnp.float32).astype(jnp.bfloat16)
        lhs[rows, LANES:] = (words >> 8).astype(jnp.float32).astype(jnp.bfloat16)

    row = lax.broadcasted_iota(jnp.int32, (2 * LANES, 2 * LANES), 0)
    col = lax.broadcasted_iota(jnp.int32, (2 * LANES, 2 * LANES), 1)
    bit = col & (BLOCK - 1)
    match = (((row >> 5) & 3) == (bit >> 4)) & ((row >> 7) == ((bit >> 3) & 1))
    factor = (1 << (7 - (bit & 7))).astype(jnp.float32) * (1.0 / 128.0)
    pattern = jnp.where(match, factor, 0.0)
    behind = (row & (GROUP - 1)) - (col >> 7)
    lane_half = lax.broadcasted_iota(jnp.int32, (BLOCK, LANES), 1) >> 6

    def two_tiles(n, carry):
        chosen = jnp.where(behind == 2 * n, pattern, 0.0).astype(jnp.bfloat16)
        raised = jnp.dot(lhs[...], chosen, preferred_element_type=jnp.float32).astype(jnp.int32)
        for r in range(replicas):
            for g in range(groups):
                for t in range(2):
                    place = g * GROUP + 2 * n + t
                    dst = meta[r, 0, place]
                    src = meta[r, 1, place]
                    column = jnp.where(src < dst_count, src, src + r * halo_blocks)
                    where = dst * pair_count + (column >> 1)
                    keep = jnp.where(lane_half == (column & 1), 1, 0)
                    first = (r * groups + g) * BLOCK
                    part = raised[first : first + BLOCK, t * LANES : (t + 1) * LANES]
                    blocks[where] += (part & keep).astype(jnp.float32)
        return carry

    lax.fori_loop(0, GROUP // 2, two_tiles, 0)

    def place_row(b, carry):
        rows = pl.ds(pl.multiple_of(b * BLOCK, BLOCK), BLOCK)
        for p in range(pair_count):
            adjacency[rows, p * LANES : (p + 1) * LANES] = blocks[b * pair_count + p].astype(
                jnp.bfloat16
            )
        return carry

    lax.fori_loop(0, dst_count, place_row, 0)

    table[:node_rows, :] = feats[...]
    for r in range(replicas):
        for first in range(0, peer_count, 8):
            part = halo[r, first : first + 8].astype(jnp.float32)
            joined = jnp.concatenate([part[:, :slots, :], part[:, slots:, :]], axis=2)
            start = node_rows + r * halo_rows + first * slots
            table[start : start + 8 * slots, :] = joined.reshape(8 * slots, width).astype(
                jnp.bfloat16
            )

    eye = lax.broadcasted_iota(jnp.int32, (LANES, LANES), 0) == lax.broadcasted_iota(
        jnp.int32, (LANES, LANES), 1
    )
    for n in range(node_rows // LANES):
        counts = norm[n : n + 1, :].astype(jnp.float32)
        column = jnp.sum(jnp.where(eye, counts, 0.0), axis=1, keepdims=True)
        scale[n * LANES : (n + 1) * LANES, :] = lax.rsqrt(column)

    def forward(q, carry):
        rows = pl.ds(pl.multiple_of(q * quarter, quarter), quarter)
        sums = jnp.dot(adjacency[rows, :], table[...], preferred_element_type=jnp.float32)
        part_scale = scale[rows, :]
        part_agg = (sums * part_scale).astype(jnp.bfloat16)
        agg[rows, :] = part_agg
        pre = jnp.dot(feats[rows, :], w_self[...], preferred_element_type=jnp.float32) + jnp.dot(
            part_agg, w_neigh[...], preferred_element_type=jnp.float32
        )
        sig = jax.nn.sigmoid(pre)

        @pl.when(q == mine)
        def _():
            out_feats[...] = (pre * sig).astype(jnp.bfloat16)

        back = (grad_out[q].astype(jnp.float32) * sig * (1.0 + pre * (1.0 - sig))).astype(
            jnp.bfloat16
        )
        grad_pre[rows, :] = back
        grad_agg[rows, :] = (times_transposed(back, w_neigh[...]) * part_scale).astype(
            jnp.bfloat16
        )
        return carry

    lax.fori_loop(0, replicas, forward, 0)

    share = width // replicas
    columns = pl.ds(pl.multiple_of(mine * share, share), share)
    weight_grad[:share, :] = transposed_times(feats[:, columns], grad_pre[...]).astype(
        jnp.bfloat16
    )
    weight_grad[share:, :] = transposed_times(agg[:, columns], grad_pre[...]).astype(jnp.bfloat16)

    for r in range(replicas):
        start = node_rows + r * halo_rows
        step = min(halo_rows, 512)
        for first in range(0, halo_rows, step):
            part = transposed_times(
                adjacency[:, start + first : start + first + step], grad_agg[...]
            )
            for n in range(step // slots):
                halo_grad[first // slots + n, r * slots : (r + 1) * slots, :] = part[
                    n * slots : (n + 1) * slots
                ].astype(jnp.bfloat16)

    own_rows = pl.ds(pl.multiple_of(mine * quarter, quarter), quarter)
    own_grad[...] = transposed_times(adjacency[:, own_rows], grad_agg[...]) + times_transposed(
        grad_pre[own_rows, :], w_self[...]
    )


def finish(
    peer_count,
    reduce_here,
    halo_grad,
    weight_grad,
    own_grad,
    targets,
    grad_feats,
    weights,
    came_halo,
    came_weight,
    summed,
    local_sem,
    halo_send,
    halo_recv,
    part_send,
    part_recv,
    full_send,
    full_recv,
    rep_send,
    rep_recv,
):
    mine_wide = lax.axis_index("wide")
    mine, core, across, diagonal = partners(4)
    enter(peer_count, mine_wide, mine, core, across)
    quarter = own_grad.shape[0]
    rows = weight_grad.shape[0] // peer_count
    per_half = peer_count // 2
    share = weight_grad.shape[0] // 2

    def push(src, dst, send, recv, wide_to, rep_to):
        copy = pltpu.make_async_remote_copy(
            src_ref=src,
            dst_ref=dst,
            send_sem=send,
            recv_sem=recv,
            device_id=(wide_to, rep_to),
            device_id_type=MESH,
        )
        copy.start()
        return copy

    def place(owner_wide, owner_rep):
        start = owner_rep * share + lax.rem(owner_wide, per_half) * rows
        return weights.at[owner_wide // per_half, pl.ds(pl.multiple_of(start, rows), rows)]

    part_copies, halo_copies, full_copies = [], [], []
    if reduce_here:
        for step in range(1, peer_count):
            peer = lax.rem(mine_wide + step, peer_count)
            piece = weight_grad.at[pl.ds(pl.multiple_of(peer * rows, rows), rows)]
            part_copies.append(
                push(
                    piece, came_weight.at[step], part_send.at[step], part_recv.at[step], peer, mine
                )
            )
    for step in range(1, peer_count):
        peer = lax.rem(mine_wide + step, peer_count)
        halo_copies.append(
            push(
                halo_grad.at[peer],
                came_halo.at[mine_wide],
                halo_send.at[step],
                halo_recv.at[step],
                peer,
                mine,
            )
        )
    kept = pltpu.make_async_copy(halo_grad.at[mine_wide], came_halo.at[mine_wide], local_sem.at[0])
    kept.start()
    if reduce_here:
        total = weight_grad[pl.ds(pl.multiple_of(mine_wide * rows, rows), rows), :].astype(
            jnp.float32
        )
        for step in range(1, peer_count):
            part_copies[step - 1].wait_recv()
            total = total + came_weight[step].astype(jnp.float32)
        summed[...] = total.astype(jnp.bfloat16)
        spot = place(mine_wide, mine)
        for step in range(1, peer_count):
            peer = lax.rem(mine_wide + step, peer_count)
            full_copies.append(
                push(summed, spot, full_send.at[step], full_recv.at[step], peer, mine)
            )
        across_copies = [
            push(summed, spot, rep_send.at[0, 0], rep_recv.at[0, 0], mine_wide, across)
        ]
        core_copies = [push(summed, spot, rep_send.at[1, 0], rep_recv.at[1, 0], mine_wide, core)]
        own_slice = pltpu.make_async_copy(summed, spot, local_sem.at[1])
        own_slice.start()

    kept.wait()
    for copy in halo_copies:
        copy.wait_recv()
    count = targets.shape[1]
    total = own_grad[...]
    block = min(count, 512)
    for first in range(0, count, block):
        chosen = targets[:, first : first + block] - mine * quarter == lax.broadcasted_iota(
            jnp.int32, (quarter, block), 0
        )
        per = block // came_halo.shape[1]
        got = came_halo[first // came_halo.shape[1] : first // came_halo.shape[1] + per].reshape(
            block, came_halo.shape[2]
        )
        total = total + jnp.dot(
            chosen.astype(jnp.bfloat16), got, preferred_element_type=jnp.float32
        )
    grad_feats[...] = total.astype(jnp.bfloat16)

    if reduce_here:
        for step in range(1, peer_count):
            full_copies[step - 1].wait_recv()
            owner = lax.rem(mine_wide + peer_count - step, peer_count)
            spot = place(owner, mine)
            across_copies.append(
                push(spot, spot, rep_send.at[0, step], rep_recv.at[0, step], mine_wide, across)
            )
            core_copies.append(
                push(spot, spot, rep_send.at[1, step], rep_recv.at[1, step], mine_wide, core)
            )
        onward = []
        for step in range(peer_count):
            across_copies[step].wait_recv()
            owner = lax.rem(mine_wide + peer_count - step, peer_count)
            spot = place(owner, across)
            onward.append(
                push(spot, spot, rep_send.at[2, step], rep_recv.at[2, step], mine_wide, core)
            )
        for copy in core_copies + onward:
            copy.wait_recv()
        for copy in part_copies + full_copies + across_copies + core_copies + onward:
            copy.wait_send()
        own_slice.wait()
    for copy in halo_copies:
        copy.wait_send()


def on_device(
    node_feats, w_self, w_neigh, send_rows, tile_dst, tile_src, tile_bits, norm_count, grad_out
):
    node_rows, width = node_feats.shape
    peer_count = lax.axis_size("wide")
    replicas = lax.axis_size("rep")
    slots = send_rows.shape[2]
    tile_total = tile_dst.shape[2]
    quarter = node_rows // replicas
    halo_rows = peer_count * slots
    halo_blocks = halo_rows // BLOCK
    words = BLOCK // 16
    groups = tile_total // GROUP

    bits = (
        tile_bits.reshape(groups, GROUP, BLOCK, words)
        .transpose(0, 2, 3, 1)
        .reshape(groups * BLOCK, words * GROUP)
    )
    send_flat = send_rows.reshape(-1)
    meta = jnp.concatenate(
        [tile_dst.reshape(1, -1), tile_src.reshape(1, -1)]
        + [jnp.zeros((6, tile_total), jnp.int32)],
        axis=0,
    )
    send_tiles = jnp.pad(send_flat, (0, -send_flat.shape[0] % (8 * LANES))).reshape(-1, LANES)
    meta = jnp.concatenate([meta, send_tiles], axis=0)
    any_spec = pl.BlockSpec(memory_space=pl.ANY)
    vmem_spec = pl.BlockSpec(memory_space=pltpu.VMEM)
    smem_spec = pl.BlockSpec(memory_space=pltpu.SMEM)

    def shaped(dims, held):
        return jax.ShapeDtypeStruct(dims, held)

    with jax.named_scope("spread_inputs"):
        all_bits, all_meta, all_grad, all_halo = pl.pallas_call(
            functools.partial(spread_inputs, peer_count, slots),
            out_shape=(
                shaped((replicas,) + bits.shape, jnp.int32),
                shaped((replicas,) + meta.shape, jnp.int32),
                shaped((replicas,) + grad_out.shape, jnp.bfloat16),
                shaped((replicas, peer_count, 2 * slots, width // 2), jnp.bfloat16),
            ),
            in_specs=[any_spec] * 3 + [vmem_spec] * 2,
            out_specs=(any_spec,) * 4,
            scratch_shapes=[
                pltpu.VMEM((peer_count, 2 * slots, width // 2), jnp.bfloat16),
                pltpu.SemaphoreType.DMA((4,)),
                pltpu.SemaphoreType.DMA((12,)),
                pltpu.SemaphoreType.DMA((12,)),
                pltpu.SemaphoreType.DMA((peer_count,)),
                pltpu.SemaphoreType.DMA((peer_count,)),
            ],
            compiler_params=pltpu.CompilerParams(
                collective_id=0, has_side_effects=True, vmem_limit_bytes=VMEM_BYTES
            ),
        )(bits, meta, grad_out, send_flat.reshape(-1, 1), node_feats)

    columns = node_rows + replicas * halo_rows
    pair_count = columns // LANES
    dst_count = node_rows // BLOCK
    with jax.named_scope("layer"):
        out_feats, own_grad, halo_grad, weight_grad = pl.pallas_call(
            functools.partial(layer, peer_count, slots),
            out_shape=(
                shaped((quarter, width), jnp.bfloat16),
                shaped((quarter, width), jnp.float32),
                shaped((peer_count, replicas * slots, width), jnp.bfloat16),
                shaped((2 * width // replicas, width), jnp.bfloat16),
            ),
            in_specs=[smem_spec] + [vmem_spec] * 7,
            out_specs=(vmem_spec,) * 4,
            scratch_shapes=[
                pltpu.VMEM((dst_count * pair_count, BLOCK, LANES), jnp.float32),
                pltpu.VMEM((node_rows, columns), jnp.bfloat16),
                pltpu.VMEM((columns, width), jnp.bfloat16),
                pltpu.VMEM((replicas * groups * BLOCK, 2 * LANES), jnp.bfloat16),
                pltpu.VMEM((node_rows, 1), jnp.float32),
                pltpu.VMEM((node_rows, width), jnp.bfloat16),
                pltpu.VMEM((node_rows, width), jnp.bfloat16),
                pltpu.VMEM((node_rows, width), jnp.bfloat16),
            ],
            compiler_params=pltpu.CompilerParams(vmem_limit_bytes=VMEM_BYTES),
        )(
            all_meta,
            all_bits,
            all_grad,
            all_halo,
            node_feats,
            w_self,
            w_neigh,
            norm_count.reshape(-1, LANES),
        )

    targets = (
        all_meta[:, 8:, :]
        .reshape(replicas, -1)[:, :halo_rows]
        .reshape(replicas, peer_count, slots)
        .transpose(1, 0, 2)
        .reshape(1, -1)
    )
    rows = weight_grad.shape[0] // peer_count
    reduce_here = rows % 16 == 0
    piece = (rows if reduce_here else 16, width)
    with jax.named_scope("finish"):
        grad_feats, weights = pl.pallas_call(
            functools.partial(finish, peer_count, reduce_here),
            out_shape=(
                shaped((quarter, width), jnp.bfloat16),
                shaped((2, width, width), jnp.bfloat16),
            ),
            in_specs=[vmem_spec] * 4,
            out_specs=(vmem_spec, any_spec),
            scratch_shapes=[
                pltpu.VMEM((peer_count, replicas * slots, width), jnp.bfloat16),
                pltpu.VMEM((peer_count,) + piece, jnp.bfloat16),
                pltpu.VMEM(piece, jnp.bfloat16),
                pltpu.SemaphoreType.DMA((2,)),
            ]
            + [pltpu.SemaphoreType.DMA((peer_count,))] * 6
            + [pltpu.SemaphoreType.DMA((3, peer_count))] * 2,
            compiler_params=pltpu.CompilerParams(
                collective_id=1, has_side_effects=True, vmem_limit_bytes=VMEM_BYTES
            ),
        )(halo_grad, weight_grad, own_grad, targets)
    if reduce_here:
        return out_feats, grad_feats, weights[0], weights[1]
    total = lax.psum(weight_grad.astype(jnp.float32), "wide").astype(jnp.bfloat16)
    whole = lax.all_gather(total, "rep", axis=0, tiled=False)
    share = width // replicas
    return (
        out_feats,
        grad_feats,
        whole[:, :share].reshape(width, width),
        whole[:, share:].reshape(width, width),
    )


def solution(mesh):
    in_specs = (
        P("wide", None),
        P(),
        P(),
        P("wide", None, "rep"),
        P("wide", "rep", None),
        P("wide", "rep", None),
        P("wide", "rep", None),
        P("wide"),
        P(("wide", "rep"), None),
    )
    out_specs = (P(("wide", "rep"), None), P(("wide", "rep"), None), P(), P())
    return jax.shard_map(
        on_device, mesh=mesh, in_specs=in_specs, out_specs=out_specs, check_vma=False
    )
```

time: 324 us -> 87.6 us (0.27)
  waiting for transfers between devices: 73.9 us -> 0 us
  Pallas kernels: 0 us -> 67.6 us
  other arithmetic: 68.9 us -> 2.53 us
  blocking collectives: 64.5 us -> 0 us
  matrix products: 44.6 us -> 0 us
  local copies, waits for them, and re-layouts: 43.5 us -> 16.4 us
  between operations: 13.9 us -> 0.7 us
  starting transfers between devices: 13 us -> 0 us
    pallas_call x0 -> x3, Pallas kernels: none -> 67.6 us  [the longest x1 28.8 us: on_device(): pl.pallas_call(functools.partial(finish, peer_count, reduce_here), out_sh...]
    psum x1 -> x0, blocking collectives: 64.5 us -> none  [on_device(): lax.psum((self_term, neigh_term), ('wide', 'rep'))]
    scatter-add x9 -> x0, other arithmetic: 56 us -> none  [the longest x4 25.9 us: forward_group(): return (running.at[dst_part].add(products), None)]
    psum x1 -> x0, waiting for transfers between devices: 51.5 us -> none  [on_device(): summed = lax.psum(partial_sum, 'rep')]
    dot_general x14 -> x0, matrix products: 44.6 us -> none  [the longest x4 17.8 us: forward_group(): jnp.einsum('tij,tjf->tif', mask_part, picked, preferred_element_type=jnp....]
    gather x9 -> x0, local copies, waits for them, and re-layouts: 28.1 us -> none  [the longest x4 13.1 us: backward_group(): picked = jnp.take(agg_blocks, dst_part, axis=0)]
    all_gather x1 -> x0, waiting for transfers between devices: 17 us -> none  [on_device(): grad_agg = lax.all_gather(own_grad_agg, 'rep', axis=0, tiled=True)]
    all_to_all x2 -> x0, starting transfers between devices: 12.8 us -> none  [the longest x1 7.28 us: on_device(): lax.all_to_all(outgoing, 'wide', split_axis=0, concat_axis=0, tiled=True)]
  transfers between devices with their start and end apart: 5 -> 0, of which waited for: 3 -> 0; matrix products, arithmetic and copies ran while one was open for 6% -> 0% of each run, Pallas kernels for 0% -> 0%
where the time goes in v1:
time: 87.6 us; the launch traced here: 87.3 us
  Pallas kernels  67.6 us (77%)
  local copies, waits for them, and re-layouts  16.4 us (19%)
  other arithmetic  2.53 us (3%)
    pallas_call x1, Pallas kernels, on_device(): pl.pallas_call(functools.partial(finish, peer_count, reduce_here), out_sh...  28.8 us
    pallas_call x1, Pallas kernels, on_device(): pl.pallas_call(functools.partial(spread_inputs, peer_count, slots), out_s...  21.1 us
    pallas_call x1, Pallas kernels, on_device(): pl.pallas_call(functools.partial(layer, peer_count, slots), out_shape=(sh...  17.7 us
    reshape x1, local copies, waits for them, and re-layouts, on_device(): tile_bits.reshape(groups, GROUP, BLOCK, words).transpose(0, 2, 3, 1)  5.65 us
    transpose x1, local copies, waits for them, and re-layouts, on_device(): bits = tile_bits.reshape(groups, GROUP, BLOCK, words).transpose(0, 2, 3,...  3.04 us
    unnamed x10, local copies, waits for them, and re-layouts  2.93 us
    squeeze x1, local copies, waits for them, and re-layouts, on_device(): return (out_feats, grad_feats, weights[0], weights[1])  2.23 us
    unnamed x1, other arithmetic  1.86 us

profile of v1, /device:TPU:0, one launch (start us, length us, event | category | flops | bytes accessed | tf_op | source)
XLA Modules:
  0.0 87.3 jit_solution(9354987233591599057)
XLA Ops:
  0.6 0.5 broadcast.7
  1.1 1.9 %reduce.3 = s32[32768]{0:T(1024)S(1)} reduce(s32[1,1,32768]{2,1,0:T(1,128)} %param.15, s32[]{:T(128)} %broadcast.7), dimensions={0,1}, to_apply=%param.15.reduce_sub_computation.3 | reduce | bytes 262148 | tf_op args[6]
  3.0 0.0 copy-start
  3.0 0.0 copy-start.1
  3.0 0.0 copy-start.2
  3.0 5.7 %reshape.38 = s32[4,32,64,4]{3,2,1,0:T(8,128)} reshape(s32[32768]{0:T(1024)S(1)} %reduce.3) | data formatting | bytes 262144 | tf_op jit(solution)/shard_map/reshape | solution.py:448
  8.7 3.0 %copy.15 = s32[4,64,4,32]{1,0,3,2:T(4,128)S(1)} copy(s32[4,64,4,32]{2,1,3,0:T(8,128)} %bitcast.18) | data formatting | bytes 262144 | tf_op jit(solution)/shard_map/transpose | solution.py:449
  11.7 0.2 reshape.39
  11.9 0.8 copy.16.bits
  12.7 0.0 copy-done
  12.7 0.7 reshape_reshape.4.index_col
  13.4 0.1 reshape.42
  13.5 0.1 pad.7.clone
  13.6 0.0 copy-done.1
  13.6 0.0 copy-done.2
  13.6 0.7 pad_add_fusion.meta
  14.2 21.1 %spread_inputs.1 = (s32[4,256,128]{2,1,0:T(8,128)}, s32[4,16,128]{2,1,0:T(8,128)}, bf16[4,256,512]{2,1,0:T(8,128)(2,1)}, bf16[4,8,16,256]{3,2,1,0:T(8,128)(2,1)}) custom-call(s32[256,128]{1,0:T(8,128)} %copy.16.bits, s32[16,128]{1,0:T(8,128)} %pad_add_fusion.meta, bf16[256,512]{1,0:T(8,128)(2,1)} %grad_out.1, s32[64,1]{1,0:T(8,128)} %reshape_reshape.4.index_col, ...), custom_call_target="tpu_custom_call" | custom-call | tf_op jit(solution)/shard_map/spread_inputs/pallas_call | solution.py:468
  35.4 17.7 %layer.1 = (bf16[256,512]{1,0:T(8,128)(2,1)}, f32[256,512]{1,0:T(8,128)}, bf16[8,32,512]{2,1,0:T(8,128)(2,1)}, bf16[256,512]{1,0:T(8,128)(2,1)}) custom-call(s32[4,16,128]{2,1,0:T(8,128)} %get-tuple-element.14.meta, s32[4,256,128]{2,1,0:T(8,128)} %get-tuple-element.15.bits, bf16[4,256,512]{2,1,0:T(8,128)(2,1)} %get-tuple-element.16.grad_out, ...), custom_call_target="tpu_custom_call" | custom-call | tf_op jit(solution)/shard_map/layer/pallas_call | solution.py:495
  53.1 0.7 slice_bitcast_fusion.2
  53.8 0.1 reshape.46
  53.9 0.7 reshape.47.targets
  54.6 28.8 %finish.1 = (bf16[256,512]{1,0:T(8,128)(2,1)}, bf16[2,512,512]{2,1,0:T(8,128)(2,1)}) custom-call(bf16[8,32,512]{2,1,0:T(8,128)(2,1)} %get-tuple-element.19.halo_grad, bf16[256,512]{1,0:T(8,128)(2,1)} %get-tuple-element.20.weight_grad, f32[256,512]{1,0:T(8,128)} %get-tuple-element.21.own_grad, s32[1,256]{1,0:T(1,128)} %reshape.47.targets), custom_call_target="tpu_custom_call" | custom-call | tf_op jit(solution)/shard_map/finish/pallas_call | solution.py:538
  83.4 2.2 %slice_bitcast_fusion = (bf16[512,512]{1,0:T(8,128)(2,1)}, bf16[512,512]{1,0:T(8,128)(2,1)}) fusion(bf16[2,512,512]{2,1,0:T(8,128)(2,1)} %get-tuple-element.23), kind=kLoop, calls=%fused_computation | loop fusion | bytes 2097152 | tf_op jit(solution)/shard_map/squeeze | solution.py:559
  85.6 1.7 %copy.23 = bf16[256,512]{1,0:T(8,128)(2,1)} copy(bf16[256,512]{1,0:T(8,128)(2,1)} %get-tuple-element.31) | data formatting | bytes 524288
  (5 shorter events, 0.0 us)
Async XLA Ops:
  3.0 9.7 %copy-start = (s32[1,8,8]{2,1,0:T(8,128)S(1)}, s32[1,8,8]{2,1,0:T(8,128)}, u32[]{:S(2)}) copy-start(s32[1,8,8]{2,1,0:T(8,128)} %param.12) | copy-start | bytes 772
  3.0 10.6 %copy-start.1 = (s32[1,1,128]{2,1,0:T(1,128)S(1)}, s32[1,1,128]{2,1,0:T(1,128)}, u32[]{:S(2)}) copy-start(s32[1,1,128]{2,1,0:T(1,128)} %param.14) | copy-start | bytes 1540
  3.0 10.5 %copy-start.2 = (s32[1,1,128]{2,1,0:T(1,128)S(1)}, s32[1,1,128]{2,1,0:T(1,128)}, u32[]{:S(2)}) copy-start(s32[1,1,128]{2,1,0:T(1,128)} %param.13) | copy-start | bytes 1540

commit v2 on v1

v2 whole, which is shorter than its diff:
```python
import functools

import jax
import jax.numpy as jnp
from jax import lax
from jax.experimental import pallas as pl
from jax.experimental.pallas import tpu as pltpu
from jax.sharding import PartitionSpec as P

BLOCK = 64
GROUP = 32
LANES = 128
MESH = pl.DeviceIdType.MESH
VMEM_BYTES = 56 * 1024 * 1024


def partners(replicas):
    mine = lax.axis_index("rep")
    core = mine + 1 - 2 * lax.rem(mine, 2)
    across = lax.rem(mine + 2, replicas)
    diagonal = lax.rem(core + 2, replicas)
    return mine, core, across, diagonal


def times_transposed(left, right):
    return lax.dot_general(
        left, right, (((1,), (1,)), ((), ())), preferred_element_type=jnp.float32
    )


def transposed_times(left, right):
    return lax.dot_general(
        left, right, (((0,), (0,)), ((), ())), preferred_element_type=jnp.float32
    )


def as_column(picks):
    count, slots = picks.shape
    same = lax.broadcasted_iota(jnp.int32, (count, slots, slots), 1) == lax.broadcasted_iota(
        jnp.int32, (count, slots, slots), 2
    )
    wide = jnp.broadcast_to(picks.astype(jnp.float32)[:, None, :], (count, slots, slots))
    column = jnp.sum(jnp.where(same, wide, 0.0), axis=2, keepdims=True)
    return column.reshape(count * slots, 1).astype(jnp.int32)


def folded(part):
    half = part.shape[1] // 2
    return jnp.concatenate([part[:, :half], part[:, half:]], axis=0).astype(jnp.bfloat16)


def unfolded(parts):
    count, rows, half = parts.shape
    wide = parts.astype(jnp.float32)
    joined = jnp.concatenate([wide[:, : rows // 2, :], wide[:, rows // 2 :, :]], axis=2)
    return joined.reshape(count * rows // 2, 2 * half).astype(jnp.bfloat16)


def sort_words(words, sorted_words):
    rows = lax.broadcasted_iota(jnp.int32, (LANES, LANES), 0)
    lanes = lax.broadcasted_iota(jnp.int32, (LANES, LANES), 1)
    wanted = (rows // GROUP) == lanes % 4
    pick_row = lax.broadcasted_iota(jnp.int32, (GROUP, 2 * LANES), 0)
    pick_lane = lax.broadcasted_iota(jnp.int32, (GROUP, 2 * LANES), 1) % LANES
    pick = jnp.where(pick_row == pick_lane // 4, 1.0, 0.0).astype(jnp.bfloat16)
    for group in range(words.shape[0] // BLOCK):
        for h in range(2):
            part = words[pl.ds(group * BLOCK + h, GROUP, stride=2), :]
            low = (part & 255).astype(jnp.float32)
            high = (part - (part & 255)).astype(jnp.float32)
            both = jnp.concatenate(
                [
                    jnp.where(wanted, jnp.concatenate([half] * 4, axis=0), 0.0)
                    for half in (low, high)
                ],
                axis=1,
            ).astype(jnp.bfloat16)
            start = group * BLOCK + h * GROUP
            sorted_words[start : start + GROUP, :] = times_transposed(pick, both).astype(jnp.int32)


def greet(peer_count, mine_wide, mine, core, across):
    barrier = pltpu.get_barrier_semaphore()
    for step in range(1, peer_count):
        peer = lax.rem(mine_wide + step, peer_count)
        pl.semaphore_signal(barrier, inc=1, device_id=(peer, mine), device_id_type=MESH)
    for other in (core, across):
        pl.semaphore_signal(barrier, inc=1, device_id=(mine_wide, other), device_id_type=MESH)
    return barrier


def push(src, dst, send, recv, wide_to, rep_to):
    copy = pltpu.make_async_remote_copy(
        src_ref=src,
        dst_ref=dst,
        send_sem=send,
        recv_sem=recv,
        device_id=(wide_to, rep_to),
        device_id_type=MESH,
    )
    copy.start()
    return copy


def spread_inputs(
    peer_count,
    slots,
    words,
    tile_dst,
    tile_src,
    send_rows,
    feats,
    all_bits,
    all_meta,
    all_halo,
    bits,
    meta,
    outgoing,
    local_sem,
    send_sem,
    recv_sem,
    halo_send,
    halo_recv,
):
    mine_wide = lax.axis_index("wide")
    mine, core, across, diagonal = partners(4)
    barrier = greet(peer_count, mine_wide, mine, core, across)
    meta[...] = jnp.zeros_like(meta)
    meta[0:1, :] = tile_dst[...]
    meta[1:2, :] = tile_src[...]
    meta[8:, :slots] = send_rows[...]
    node_rows = feats.shape[0]
    for first in range(0, peer_count, 8):
        picks = as_column(send_rows[first : first + 8, :])
        chosen = picks == lax.broadcasted_iota(jnp.int32, (8 * slots, node_rows), 1)
        rows = jnp.dot(
            jnp.where(chosen, 1.0, 0.0).astype(jnp.bfloat16),
            feats[...],
            preferred_element_type=jnp.float32,
        )
        for n in range(8):
            outgoing[first + n] = folded(rows[n * slots : (n + 1) * slots])
    sort_words(words, bits)
    pl.semaphore_wait(barrier, peer_count + 1)

    exchange = []
    for step in range(1, peer_count):
        peer = lax.rem(mine_wide + step, peer_count)
        exchange.append(
            push(
                outgoing.at[peer],
                all_halo.at[mine, mine_wide],
                halo_send.at[step],
                halo_recv.at[step],
                peer,
                mine,
            )
        )
    pairs = ((bits, all_bits), (meta, all_meta))
    to_across = [
        push(src, dst.at[mine], send_sem.at[n], recv_sem.at[n], mine_wide, across)
        for n, (src, dst) in enumerate(pairs)
    ]
    to_core = [
        push(src, dst.at[mine], send_sem.at[3 + n], recv_sem.at[3 + n], mine_wide, core)
        for n, (src, dst) in enumerate(pairs)
    ]
    own = [
        pltpu.make_async_copy(src, dst.at[mine], local_sem.at[n])
        for n, (src, dst) in enumerate(pairs)
    ]
    kept = pltpu.make_async_copy(
        outgoing.at[mine_wide], all_halo.at[mine, mine_wide], local_sem.at[2]
    )
    for copy in own + [kept]:
        copy.start()
    kept.wait()
    for copy in exchange:
        copy.wait_recv()
    block = all_halo.at[mine]
    to_across.append(push(block, block, send_sem.at[2], recv_sem.at[2], mine_wide, across))
    to_core.append(push(block, block, send_sem.at[5], recv_sem.at[5], mine_wide, core))
    onward = []
    for n, dst in enumerate((all_bits, all_meta, all_halo)):
        to_across[n].wait_recv()
        block = dst.at[across]
        onward.append(push(block, block, send_sem.at[6 + n], recv_sem.at[6 + n], mine_wide, core))
    for copy in to_core + onward:
        copy.wait_recv()
    for copy in to_across + to_core + onward + exchange:
        copy.wait_send()
    for copy in own:
        copy.wait()


def build_adjacency(dst_count, halo_blocks, meta, bits, adjacency, blocks, lhs):
    replicas = bits.shape[0]
    pair_count = (dst_count + replicas * halo_blocks) // 2
    groups = bits.shape[1] // BLOCK

    blocks[...] = jnp.zeros_like(blocks)
    for r in range(replicas):
        words = bits[r]
        rows = pl.ds(r * words.shape[0], words.shape[0])
        lhs[rows, :LANES] = (words & 255).astype(jnp.float32).astype(jnp.bfloat16)
        lhs[rows, LANES:] = (words >> 8).astype(jnp.float32).astype(jnp.bfloat16)

    row = lax.broadcasted_iota(jnp.int32, (2 * LANES, 2 * LANES), 0)
    col = lax.broadcasted_iota(jnp.int32, (2 * LANES, 2 * LANES), 1)
    bit = col & (BLOCK - 1)
    match = (((row >> 5) & 3) == (bit >> 4)) & ((row >> 7) == ((bit >> 3) & 1))
    factor = (1 << (7 - (bit & 7))).astype(jnp.float32) * (1.0 / 128.0)
    pattern = jnp.where(match, factor, 0.0)
    behind = (row & (GROUP - 1)) - (col >> 7)
    lane_half = lax.broadcasted_iota(jnp.int32, (BLOCK, LANES), 1) >> 6

    def two_tiles(n, carry):
        chosen = jnp.where(behind == 2 * n, pattern, 0.0).astype(jnp.bfloat16)
        raised = jnp.dot(lhs[...], chosen, preferred_element_type=jnp.float32).astype(jnp.int32)
        for r in range(replicas):
            for g in range(groups):
                for t in range(2):
                    place = g * GROUP + 2 * n + t
                    dst = meta[r, 0, place]
                    src = meta[r, 1, place]
                    column = jnp.where(src < dst_count, src, src + r * halo_blocks)
                    where = dst * pair_count + (column >> 1)
                    keep = jnp.where(lane_half == (column & 1), 1, 0)
                    first = (r * groups + g) * BLOCK
                    part = raised[first : first + BLOCK, t * LANES : (t + 1) * LANES]
                    blocks[where] += (part & keep).astype(jnp.float32)
        return carry

    lax.fori_loop(0, GROUP // 2, two_tiles, 0)

    def place_row(b, carry):
        rows = pl.ds(pl.multiple_of(b * BLOCK, BLOCK), BLOCK)
        for p in range(pair_count):
            adjacency[rows, p * LANES : (p + 1) * LANES] = blocks[b * pair_count + p].astype(
                jnp.bfloat16
            )
        return carry

    lax.fori_loop(0, dst_count, place_row, 0)


def layer(
    peer_count,
    slots,
    reduce_here,
    adjacency,
    halo,
    meta,
    grad_own,
    grad_core,
    grad_across,
    grad_diagonal,
    feats,
    w_self,
    w_neigh,
    norm,
    out_feats,
    grad_feats,
    weights,
    weight_grad,
    table,
    scale,
    agg,
    grad_pre,
    grad_agg,
    halo_grad,
    halo_out,
    came_halo,
    came_weight,
    summed,
    local_sem,
    halo_send,
    halo_recv,
    part_send,
    part_recv,
    full_send,
    full_recv,
    rep_send,
    rep_recv,
    back_send,
    back_recv,
):
    mine_wide = lax.axis_index("wide")
    mine, core, across, diagonal = partners(4)
    barrier = greet(peer_count, mine_wide, mine, core, across)
    replicas = halo.shape[0]
    node_rows, width = feats.shape
    halo_rows = peer_count * slots
    quarter = node_rows // replicas
    share = width // replicas
    rows = 2 * share // peer_count
    per_half = peer_count // 2

    table[:node_rows, :] = feats[...]
    for r in range(replicas):
        for first in range(0, peer_count, 8):
            start = node_rows + r * halo_rows + first * slots
            table[start : start + 8 * slots, :] = unfolded(halo[r, first : first + 8])
    eye = lax.broadcasted_iota(jnp.int32, (LANES, LANES), 0) == lax.broadcasted_iota(
        jnp.int32, (LANES, LANES), 1
    )
    for n in range(node_rows // LANES):
        counts = norm[n : n + 1, :].astype(jnp.float32)
        column = jnp.sum(jnp.where(eye, counts, 0.0), axis=1, keepdims=True)
        scale[n * LANES : (n + 1) * LANES, :] = lax.rsqrt(column)

    def rows_of(q):
        return pl.ds(pl.multiple_of(q * quarter, quarter), quarter)

    parts = ((mine, grad_own), (core, grad_core), (across, grad_across), (diagonal, grad_diagonal))
    for q, grad_out in parts:
        here = rows_of(q)
        sums = jnp.dot(adjacency[here, :], table[...], preferred_element_type=jnp.float32)
        part_scale = scale[here, :]
        part_agg = (sums * part_scale).astype(jnp.bfloat16)
        agg[here, :] = part_agg
        pre = jnp.dot(feats[here, :], w_self[...], preferred_element_type=jnp.float32) + jnp.dot(
            part_agg, w_neigh[...], preferred_element_type=jnp.float32
        )
        sig = jax.nn.sigmoid(pre)
        if grad_out is grad_own:
            out_feats[...] = (pre * sig).astype(jnp.bfloat16)
        back = (grad_out[...].astype(jnp.float32) * sig * (1.0 + pre * (1.0 - sig))).astype(
            jnp.bfloat16
        )
        grad_pre[here, :] = back
        grad_agg[here, :] = (times_transposed(back, w_neigh[...]) * part_scale).astype(
            jnp.bfloat16
        )

    columns = pl.ds(pl.multiple_of(mine * share, share), share)
    weight_grad[:share, :] = transposed_times(feats[:, columns], grad_pre[...]).astype(
        jnp.bfloat16
    )
    weight_grad[share:, :] = transposed_times(agg[:, columns], grad_pre[...]).astype(jnp.bfloat16)
    pl.semaphore_wait(barrier, peer_count + 1)

    def place(owner_wide, owner_rep):
        start = owner_rep * share + lax.rem(owner_wide, per_half) * rows
        return weights.at[owner_wide // per_half, pl.ds(pl.multiple_of(start, rows), rows)]

    part_copies, halo_copies, full_copies = [], [], []
    if reduce_here:
        for step in range(1, peer_count):
            peer = lax.rem(mine_wide + step, peer_count)
            piece = weight_grad.at[pl.ds(pl.multiple_of(peer * rows, rows), rows)]
            part_copies.append(
                push(
                    piece, came_weight.at[step], part_send.at[step], part_recv.at[step], peer, mine
                )
            )

    block = min(replicas * halo_rows, 512)
    for first in range(0, replicas * halo_rows, block):
        start = node_rows + first
        halo_grad[first : first + block, :] = transposed_times(
            adjacency[:, start : start + block], grad_agg[...]
        )
    for n in range(peer_count):
        start = pl.multiple_of(mine * halo_rows, 8) + n * slots
        halo_out[n] = folded(halo_grad[pl.ds(pl.multiple_of(start, 8), slots), :])
    for step in range(1, peer_count):
        peer = lax.rem(mine_wide + step, peer_count)
        halo_copies.append(
            push(
                halo_out.at[peer],
                came_halo.at[mine, mine_wide],
                halo_send.at[step],
                halo_recv.at[step],
                peer,
                mine,
            )
        )
    kept = pltpu.make_async_copy(
        halo_out.at[mine_wide], came_halo.at[mine, mine_wide], local_sem.at[0]
    )
    kept.start()
    own_rows = rows_of(mine)
    total_grad = transposed_times(adjacency[:, own_rows], grad_agg[...]) + times_transposed(
        grad_pre[own_rows, :], w_self[...]
    )

    if reduce_here:
        total = weight_grad[pl.ds(pl.multiple_of(mine_wide * rows, rows), rows), :].astype(
            jnp.float32
        )
        for step in range(1, peer_count):
            part_copies[step - 1].wait_recv()
            total = total + came_weight[step].astype(jnp.float32)
        summed[...] = total.astype(jnp.bfloat16)
        spot = place(mine_wide, mine)
        for step in range(1, peer_count):
            peer = lax.rem(mine_wide + step, peer_count)
            full_copies.append(
                push(summed, spot, full_send.at[step], full_recv.at[step], peer, mine)
            )
        across_copies = [
            push(summed, spot, rep_send.at[0, 0], rep_recv.at[0, 0], mine_wide, across)
        ]
        core_copies = [push(summed, spot, rep_send.at[1, 0], rep_recv.at[1, 0], mine_wide, core)]
        own_slice = pltpu.make_async_copy(summed, spot, local_sem.at[1])
        own_slice.start()

    kept.wait()
    for copy in halo_copies:
        copy.wait_recv()
    block = came_halo.at[mine]
    back_across = push(block, block, back_send.at[0], back_recv.at[0], mine_wide, across)
    back_core = push(block, block, back_send.at[1], back_recv.at[1], mine_wide, core)

    if reduce_here:
        for step in range(1, peer_count):
            full_copies[step - 1].wait_recv()
            owner = lax.rem(mine_wide + peer_count - step, peer_count)
            spot = place(owner, mine)
            across_copies.append(
                push(spot, spot, rep_send.at[0, step], rep_recv.at[0, step], mine_wide, across)
            )
            core_copies.append(
                push(spot, spot, rep_send.at[1, step], rep_recv.at[1, step], mine_wide, core)
            )

    back_across.wait_recv()
    block = came_halo.at[across]
    back_onward = push(block, block, back_send.at[2], back_recv.at[2], mine_wide, core)
    back_core.wait_recv()
    back_onward.wait_recv()
    for r in range(replicas):
        for first in range(0, peer_count, 8):
            picks = as_column(meta[r, 8 + first : 16 + first, :slots]) - mine * quarter
            chosen = picks == lax.broadcasted_iota(jnp.int32, (8 * slots, quarter), 1)
            total_grad = total_grad + transposed_times(
                jnp.where(chosen, 1.0, 0.0).astype(jnp.bfloat16),
                unfolded(came_halo[r, first : first + 8]),
            )
    grad_feats[...] = total_grad.astype(jnp.bfloat16)

    if reduce_here:
        onward = []
        for step in range(peer_count):
            across_copies[step].wait_recv()
            owner = lax.rem(mine_wide + peer_count - step, peer_count)
            spot = place(owner, across)
            onward.append(
                push(spot, spot, rep_send.at[2, step], rep_recv.at[2, step], mine_wide, core)
            )
        for copy in core_copies + onward:
            copy.wait_recv()
        for copy in part_copies + full_copies + across_copies + core_copies + onward:
            copy.wait_send()
        own_slice.wait()
    for copy in halo_copies + [back_across, back_core, back_onward]:
        copy.wait_send()


def on_device(
    node_feats, w_self, w_neigh, send_rows, tile_dst, tile_src, tile_bits, norm_count, grad_out
):
    node_rows, width = node_feats.shape
    peer_count = lax.axis_size("wide")
    replicas = lax.axis_size("rep")
    slots = send_rows.shape[2]
    tile_total = tile_dst.shape[2]
    quarter = node_rows // replicas
    halo_rows = peer_count * slots
    halo_blocks = halo_rows // BLOCK
    words = tile_bits.reshape(-1, LANES)
    any_spec = pl.BlockSpec(memory_space=pl.ANY)
    vmem_spec = pl.BlockSpec(memory_space=pltpu.VMEM)
    smem_spec = pl.BlockSpec(memory_space=pltpu.SMEM)

    def shaped(dims, held):
        return jax.ShapeDtypeStruct(dims, held)

    def dma(*dims):
        return pltpu.SemaphoreType.DMA(dims)

    by_core = [(n, n + 1 - 2 * (n % 2)) for n in range(replicas)]
    by_chip = [(n, (n + 2) % replicas) for n in range(replicas)]
    grad_across = lax.ppermute(grad_out, "rep", by_chip)
    grad_core = lax.ppermute(grad_out, "rep", by_core)
    grad_diagonal = lax.ppermute(grad_across, "rep", by_core)

    halo_shape = (replicas, peer_count, 2 * slots, width // 2)
    meta_shape = (8 + peer_count, tile_total)
    with jax.named_scope("spread_inputs"):
        all_bits, all_meta, all_halo = pl.pallas_call(
            functools.partial(spread_inputs, peer_count, slots),
            out_shape=(
                shaped((replicas,) + words.shape, jnp.int32),
                shaped((replicas,) + meta_shape, jnp.int32),
                shaped(halo_shape, jnp.bfloat16),
            ),
            in_specs=[vmem_spec] * 5,
            out_specs=(any_spec,) * 3,
            scratch_shapes=[
                pltpu.VMEM(words.shape, jnp.int32),
                pltpu.VMEM(meta_shape, jnp.int32),
                pltpu.VMEM(halo_shape[1:], jnp.bfloat16),
                dma(3),
                dma(9),
                dma(9),
                dma(peer_count),
                dma(peer_count),
            ],
            compiler_params=pltpu.CompilerParams(
                collective_id=0, has_side_effects=True, vmem_limit_bytes=VMEM_BYTES
            ),
        )(words, tile_dst[0], tile_src[0], send_rows[0], node_feats)

    columns = node_rows + replicas * halo_rows
    pair_count = columns // LANES
    dst_count = node_rows // BLOCK
    with jax.named_scope("build_adjacency"):
        adjacency = pl.pallas_call(
            functools.partial(build_adjacency, dst_count, halo_blocks),
            out_shape=shaped((node_rows, columns), jnp.bfloat16),
            in_specs=[smem_spec, vmem_spec],
            out_specs=vmem_spec,
            scratch_shapes=[
                pltpu.VMEM((dst_count * pair_count, BLOCK, LANES), jnp.float32),
                pltpu.VMEM((replicas * words.shape[0], 2 * LANES), jnp.bfloat16),
            ],
            compiler_params=pltpu.CompilerParams(vmem_limit_bytes=VMEM_BYTES),
            cost_estimate=pl.CostEstimate(
                flops=8 * 10**9, bytes_accessed=4 * 10**6, transcendentals=0
            ),
        )(all_meta, all_bits)

    rows = 2 * width // replicas // peer_count
    reduce_here = rows % 16 == 0
    piece = (rows if reduce_here else 16, width)
    with jax.named_scope("layer"):
        out_feats, grad_feats, weights, weight_grad = pl.pallas_call(
            functools.partial(layer, peer_count, slots, reduce_here),
            out_shape=(
                shaped((quarter, width), jnp.bfloat16),
                shaped((quarter, width), jnp.bfloat16),
                shaped((2, width, width), jnp.bfloat16),
                shaped((2 * width // replicas, width), jnp.bfloat16),
            ),
            in_specs=[vmem_spec] * 11,
            out_specs=(vmem_spec, vmem_spec, any_spec, vmem_spec),
            scratch_shapes=[
                pltpu.VMEM((columns, width), jnp.bfloat16),
                pltpu.VMEM((node_rows, 1), jnp.float32),
                pltpu.VMEM((node_rows, width), jnp.bfloat16),
                pltpu.VMEM((node_rows, width), jnp.bfloat16),
                pltpu.VMEM((node_rows, width), jnp.bfloat16),
                pltpu.VMEM((replicas * halo_rows, width), jnp.float32),
                pltpu.VMEM(halo_shape[1:], jnp.bfloat16),
                pltpu.VMEM(halo_shape, jnp.bfloat16),
                pltpu.VMEM((peer_count,) + piece, jnp.bfloat16),
                pltpu.VMEM(piece, jnp.bfloat16),
                dma(2),
            ]
            + [dma(peer_count)] * 6
            + [dma(3, peer_count)] * 2
            + [dma(3)] * 2,
            compiler_params=pltpu.CompilerParams(
                collective_id=1, has_side_effects=True, vmem_limit_bytes=VMEM_BYTES
            ),
        )(
            adjacency,
            all_halo,
            all_meta,
            grad_out,
            grad_core,
            grad_across,
            grad_diagonal,
            node_feats,
            w_self,
            w_neigh,
            norm_count.reshape(-1, LANES),
        )
    if reduce_here:
        return out_feats, grad_feats, weights[0], weights[1]
    total = lax.psum(weight_grad.astype(jnp.float32), "wide").astype(jnp.bfloat16)
    whole = lax.all_gather(total, "rep", axis=0, tiled=False)
    share = width // replicas
    return (
        out_feats,
        grad_feats,
        whole[:, :share].reshape(width, width),
        whole[:, share:].reshape(width, width),
    )


def solution(mesh):
    in_specs = (
        P("wide", None),
        P(),
        P(),
        P("wide", None, "rep"),
        P("wide", "rep", None),
        P("wide", "rep", None),
        P("wide", "rep", None),
        P("wide"),
        P(("wide", "rep"), None),
    )
    out_specs = (P(("wide", "rep"), None), P(("wide", "rep"), None), P(), P())
    return jax.shard_map(
        on_device, mesh=mesh, in_specs=in_specs, out_specs=out_specs, check_vma=False
    )
```

time: 87.6 us -> 65.4 us (0.75)
  Pallas kernels: 67.6 us -> 55.6 us
  local copies, waits for them, and re-layouts: 16.4 us -> 5.42 us
  starting transfers between devices: 0 us -> 3.44 us
  other arithmetic: 2.53 us -> 0 us
    reshape x7 -> x0, local copies, waits for them, and re-layouts: 7.46 us -> none  [the longest x1 5.65 us: on_device(): tile_bits.reshape(groups, GROUP, BLOCK, words).transpose(0, 2, 3, 1)]
    pallas_call x1, Pallas kernels: 21.1 us -> 13.8 us  [on_device(): pl.pallas_call(functools.partial(spread_inputs, peer_count, slots), out_s...]
    pallas_call x2, Pallas kernels: 46.5 us -> 41.8 us  [the longest x1 31.2 us: on_device(): pl.pallas_call(functools.partial(layer, peer_count, slots, reduce_here),...]
    ppermute x0 -> x3, starting transfers between devices: none -> 3.44 us  [the longest x1 3 us: on_device(): grad_across = lax.ppermute(grad_out, 'rep', by_chip)]
    transpose x2 -> x0, local copies, waits for them, and re-layouts: 3.04 us -> none  [the longest x1 3.04 us: on_device(): bits = tile_bits.reshape(groups, GROUP, BLOCK, words).transpose(0, 2, 3,...]
    unnamed x1 -> x0, other arithmetic: 1.86 us -> none
  transfers between devices with their start and end apart: 0 -> 3, of which waited for: 0 -> 0; matrix products, arithmetic and copies ran while one was open for 0% -> 0% of each run, Pallas kernels for 0% -> 37%
where the time goes in v2:
time: 65.4 us; the launch traced here: 65.2 us
  Pallas kernels  55.6 us (85%)
  local copies, waits for them, and re-layouts  5.42 us (8%)
  starting transfers between devices  3.44 us (5%)
  between operations  0.7 us (1%)
    pallas_call x1, Pallas kernels, on_device(): pl.pallas_call(functools.partial(layer, peer_count, slots, reduce_here),...  31.2 us
    pallas_call x1, Pallas kernels, on_device(): pl.pallas_call(functools.partial(spread_inputs, peer_count, slots), out_s...  13.8 us
    pallas_call x1, Pallas kernels, on_device(): pl.pallas_call(functools.partial(build_adjacency, dst_count, halo_blocks)...  10.5 us
    unnamed x10, local copies, waits for them, and re-layouts  3.15 us
    ppermute x1, starting transfers between devices, on_device(): grad_across = lax.ppermute(grad_out, 'rep', by_chip)  3 us
    squeeze x1, local copies, waits for them, and re-layouts, on_device(): return (out_feats, grad_feats, weights[0], weights[1])  2.28 us
  transfers between devices with their start and end apart: 3, of which 0 were waited for; matrix products, arithmetic and copies ran while one was open for 0% of the time, Pallas kernels for 37%

profile of v2, /device:TPU:0, one launch (start us, length us, event | category | flops | bytes accessed | tf_op | source)
XLA Modules:
  0.0 65.2 jit_solution(17774294625020226786)
XLA Ops:
  0.6 3.0 %collective-permute-start.1 = (bf16[256,512]{1,0:T(8,128)(2,1)}, bf16[256,512]{1,0:T(8,128)(2,1)S(1)}, u32[]{:S(2)}, u32[]{:S(2)}) collective-permute-start(bf16[256,512]{1,0:T(8,128)(2,1)} %grad_own.1), channel_id=1, source_target_pairs={{0,2},{1,3},{2,0},{3,1},{4,6},{5,7},{6,4},{7,5},{8,10},{9,11},{10,... | collective-permute-start | bytes 786440 | tf_op jit(solution)/shard_map/ppermute | solution.py:485
  3.6 0.0 collective-permute-start
  3.6 13.8 %spread_inputs.1 = (s32[4,256,128]{2,1,0:T(8,128)}, s32[4,16,128]{2,1,0:T(8,128)}, bf16[4,8,16,256]{3,2,1,0:T(8,128)(2,1)}) custom-call(s32[256,128]{1,0:T(8,128)} %bitcast.9, s32[1,128]{1,0:T(1,128)} %bitcast.12, s32[1,128]{1,0:T(1,128)} %bitcast.13, s32[8,8]{1,0:T(8,128)} %bitcast.10, bf16[1024,512]{1,0:T(8,128)(2,1)} %feats.3), custom_call_target="tpu_custom_call" | custom-call | tf_op jit(solution)/shard_map/spread_inputs/pallas_call | solution.py:492
  17.5 0.0 collective-permute-done.1.grad_across
  17.5 0.0 copy-start.1
  17.5 0.4 collective-permute-start.2
  17.9 10.5 %build_adjacency.1.adjacency = bf16[1024,1280]{1,0:T(8,128)(2,1)} custom-call(s32[4,16,128]{2,1,0:T(8,128)} %get-tuple-element.10.meta, s32[4,256,128]{2,1,0:T(8,128)} %get-tuple-element.11.bits), custom_call_target="tpu_custom_call" | custom-call | flops 8000000000 | bytes 4000000 | tf_op jit(solution)/shard_map/build_adjacency/pallas_call | solution.py:520
  28.4 0.0 copy-done.1
  28.4 0.0 collective-permute-done.grad_core
  28.4 0.0 copy-start.2
  28.5 0.0 collective-permute-done.2.grad_diagonal
  28.5 0.0 copy-start.3
  28.5 0.7 %copy-done.2 = bf16[256,512]{1,0:T(8,128)(2,1)} copy-done((bf16[256,512]{1,0:T(8,128)(2,1)}, bf16[256,512]{1,0:T(8,128)(2,1)S(1)}, u32[]{:S(2)}) %copy-start.2) | copy-done | bytes 262168
  29.2 0.1 copy-done.3
  29.2 31.2 %layer.1 = (bf16[256,512]{1,0:T(8,128)(2,1)}, bf16[256,512]{1,0:T(8,128)(2,1)}, bf16[2,512,512]{2,1,0:T(8,128)(2,1)}, bf16[256,512]{1,0:T(8,128)(2,1)}) custom-call(bf16[1024,1280]{1,0:T(8,128)(2,1)} %build_adjacency.1.adjacency, bf16[4,8,16,256]{3,2,1,0:T(8,128)(2,1)} %get-tuple-element.12.halo, s32[4,16,128]{2,1,0:T(8,128)} %get-tuple-element.10.meta, ...), custom_call_target="tpu_custom_call" | custom-call | tf_op jit(solution)/shard_map/layer/pallas_call | solution.py:539
  60.5 0.0 copy-start
  60.5 2.3 %slice_bitcast_fusion = (bf16[512,512]{1,0:T(8,128)(2,1)}, bf16[512,512]{1,0:T(8,128)(2,1)}) fusion(bf16[2,512,512]{2,1,0:T(8,128)(2,1)} %get-tuple-element.15), kind=kLoop, calls=%fused_computation | loop fusion | bytes 2097152 | tf_op jit(solution)/shard_map/squeeze | solution.py:582
  62.8 1.7 %copy.15 = bf16[256,512]{1,0:T(8,128)(2,1)} copy(bf16[256,512]{1,0:T(8,128)(2,1)} %get-tuple-element.22) | data formatting | bytes 524288
  64.4 0.0 copy-done
  64.4 0.7 %copy.16 = bf16[256,512]{1,0:T(8,128)(2,1)} copy(bf16[256,512]{1,0:T(8,128)(2,1)S(1)} %copy-done) | data formatting | bytes 524288
Async XLA Ops:
  0.6 16.8 %collective-permute-start.1 = (bf16[256,512]{1,0:T(8,128)(2,1)}, bf16[256,512]{1,0:T(8,128)(2,1)S(1)}, u32[]{:S(2)}, u32[]{:S(2)}) collective-permute-start(bf16[256,512]{1,0:T(8,128)(2,1)} %grad_own.1), channel_id=1, source_target_pairs={{0,2},{1,3},{2,0},{3,1},{4,6},{5,7},{6,4},{7,5},{8,10},{9,11},{10,... | collective-permute-start | bytes 786440 | tf_op jit(solution)/shard_map/ppermute | solution.py:485
  3.6 24.8 %collective-permute-start = (bf16[256,512]{1,0:T(8,128)(2,1)}, bf16[256,512]{1,0:T(8,128)(2,1)S(1)}, u32[]{:S(2)}, u32[]{:S(2)}) collective-permute-start(bf16[256,512]{1,0:T(8,128)(2,1)} %grad_own.1), channel_id=1, source_target_pairs={{0,1},{1,0},{2,3},{3,2},{4,5},{5,4},{6,7},{7,6},{8,9},{9,8},{10,11... | collective-permute-start | bytes 786440 | tf_op jit(solution)/shard_map/ppermute | solution.py:486
  17.5 11.0 %copy-start.1 = (bf16[256,512]{1,0:T(8,128)(2,1)}, bf16[256,512]{1,0:T(8,128)(2,1)S(1)}, u32[]{:S(2)}) copy-start(bf16[256,512]{1,0:T(8,128)(2,1)S(1)} %collective-permute-done.1.grad_across) | copy-start | bytes 786436
  17.5 11.0 %collective-permute-start.2 = (bf16[256,512]{1,0:T(8,128)(2,1)S(1)}, bf16[256,512]{1,0:T(8,128)(2,1)S(1)}, u32[]{:S(2)}, u32[]{:S(2)}) collective-permute-start(bf16[256,512]{1,0:T(8,128)(2,1)S(1)} %collective-permute-done.1.grad_across), channel_id=1, source_target_pairs={{0,1},{1,0},{2,3},{3,2},{4,5},{5,4},{6,7},{7,6},{8,9},{9,8},{10,11... | collective-permute-start | bytes 786440 | tf_op jit(solution)/shard_map/ppermute | solution.py:487
  28.4 0.7 %copy-start.2 = (bf16[256,512]{1,0:T(8,128)(2,1)}, bf16[256,512]{1,0:T(8,128)(2,1)S(1)}, u32[]{:S(2)}) copy-start(bf16[256,512]{1,0:T(8,128)(2,1)S(1)} %collective-permute-done.grad_core) | copy-start | bytes 786436
  28.5 0.8 %copy-start.3 = (bf16[256,512]{1,0:T(8,128)(2,1)}, bf16[256,512]{1,0:T(8,128)(2,1)S(1)}, u32[]{:S(2)}) copy-start(bf16[256,512]{1,0:T(8,128)(2,1)S(1)} %collective-permute-done.2.grad_diagonal) | copy-start | bytes 786436
  60.5 4.0 %copy-start = (bf16[256,512]{1,0:T(8,128)(2,1)S(1)}, bf16[256,512]{1,0:T(8,128)(2,1)}, u32[]{:S(2)}) copy-start(bf16[256,512]{1,0:T(8,128)(2,1)} %get-tuple-element.23) | copy-start | bytes 786436

commit v3 on v2

--- a/solution.py
+++ b/solution.py
@@ -112,7 +112,7 @@
     feats,
     all_bits,
     all_meta,
-    all_halo,
+    halo,
     bits,
     meta,
     outgoing,
@@ -149,7 +149,7 @@
         exchange.append(
             push(
                 outgoing.at[peer],
-                all_halo.at[mine, mine_wide],
+                halo.at[mine_wide],
                 halo_send.at[step],
                 halo_recv.at[step],
                 peer,
@@ -169,23 +169,17 @@
         pltpu.make_async_copy(src, dst.at[mine], local_sem.at[n])
         for n, (src, dst) in enumerate(pairs)
     ]
-    kept = pltpu.make_async_copy(
-        outgoing.at[mine_wide], all_halo.at[mine, mine_wide], local_sem.at[2]
-    )
-    for copy in own + [kept]:
+    own.append(
+        pltpu.make_async_copy(outgoing.at[mine_wide], halo.at[mine_wide], local_sem.at[2])
+    )
+    for copy in own:
         copy.start()
-    kept.wait()
-    for copy in exchange:
-        copy.wait_recv()
-    block = all_halo.at[mine]
-    to_across.append(push(block, block, send_sem.at[2], recv_sem.at[2], mine_wide, across))
-    to_core.append(push(block, block, send_sem.at[5], recv_sem.at[5], mine_wide, core))
     onward = []
-    for n, dst in enumerate((all_bits, all_meta, all_halo)):
+    for n, dst in enumerate((all_bits, all_meta)):
         to_across[n].wait_recv()
         block = dst.at[across]
         onward.append(push(block, block, send_sem.at[6 + n], recv_sem.at[6 + n], mine_wide, core))
-    for copy in to_core + onward:
+    for copy in to_core + onward + exchange:
         copy.wait_recv()
     for copy in to_across + to_core + onward + exchange:
         copy.wait_send()
@@ -193,12 +187,19 @@
         copy.wait()
 
 
-def build_adjacency(dst_count, halo_blocks, meta, bits, adjacency, blocks, lhs):
+def build_adjacency(
+    dst_count, halo_blocks, meta, bits, adjacency, low_sum, high_sum, lhs, raised_even, raised_odd
+):
     replicas = bits.shape[0]
-    pair_count = (dst_count + replicas * halo_blocks) // 2
+    per_sum = replicas // 2
+    own_pairs = dst_count // 2
+    halo_pairs = per_sum * halo_blocks // 2
+    pair_count = own_pairs + halo_pairs
     groups = bits.shape[1] // BLOCK
-
-    blocks[...] = jnp.zeros_like(blocks)
+    sums = (low_sum, high_sum)
+
+    for target in sums:
+        target[...] = jnp.zeros_like(target)
     for r in range(replicas):
         words = bits[r]
         rows = pl.ds(r * words.shape[0], words.shape[0])
@@ -214,31 +215,49 @@
     behind = (row & (GROUP - 1)) - (col >> 7)
     lane_half = lax.broadcasted_iota(jnp.int32, (BLOCK, LANES), 1) >> 6
 
-    def two_tiles(n, carry):
+    def expand(n):
         chosen = jnp.where(behind == 2 * n, pattern, 0.0).astype(jnp.bfloat16)
-        raised = jnp.dot(lhs[...], chosen, preferred_element_type=jnp.float32).astype(jnp.int32)
-        for r in range(replicas):
-            for g in range(groups):
-                for t in range(2):
+        return jnp.dot(lhs[...], chosen, preferred_element_type=jnp.float32)
+
+    def add_tiles(raised, n):
+        for g in range(groups):
+            for t in range(2):
+                for turn in range(replicas):
+                    r = (turn % 2) * per_sum + turn // 2
                     place = g * GROUP + 2 * n + t
                     dst = meta[r, 0, place]
                     src = meta[r, 1, place]
-                    column = jnp.where(src < dst_count, src, src + r * halo_blocks)
+                    column = jnp.where(src < dst_count, src, src + (r % per_sum) * halo_blocks)
                     where = dst * pair_count + (column >> 1)
                     keep = jnp.where(lane_half == (column & 1), 1, 0)
                     first = (r * groups + g) * BLOCK
                     part = raised[first : first + BLOCK, t * LANES : (t + 1) * LANES]
-                    blocks[where] += (part & keep).astype(jnp.float32)
+                    sums[r // per_sum][where] += (
+                        (part.astype(jnp.int32) & keep).astype(jnp.float32).astype(jnp.bfloat16)
+                    )
+
+    raised_even[...] = expand(0)
+
+    def four_tiles(m, carry):
+        raised_odd[...] = expand(2 * m + 1)
+        add_tiles(raised_even, 2 * m)
+        raised_even[...] = expand(2 * m + 2)
+        add_tiles(raised_odd, 2 * m + 1)
         return carry
 
-    lax.fori_loop(0, GROUP // 2, two_tiles, 0)
+    lax.fori_loop(0, GROUP // 4, four_tiles, 0)
 
     def place_row(b, carry):
         rows = pl.ds(pl.multiple_of(b * BLOCK, BLOCK), BLOCK)
-        for p in range(pair_count):
-            adjacency[rows, p * LANES : (p + 1) * LANES] = blocks[b * pair_count + p].astype(
-                jnp.bfloat16
-            )
+        for p in range(own_pairs):
+            both = low_sum[b * pair_count + p].astype(jnp.float32) + high_sum[
+                b * pair_count + p
+            ].astype(jnp.float32)
+            adjacency[rows, p * LANES : (p + 1) * LANES] = both.astype(jnp.bfloat16)
+        for n, target in enumerate(sums):
+            for p in range(halo_pairs):
+                start = (own_pairs + n * halo_pairs + p) * LANES
+                adjacency[rows, start : start + LANES] = target[b * pair_count + own_pairs + p]
         return carry
 
     lax.fori_loop(0, dst_count, place_row, 0)
@@ -249,7 +268,10 @@
     slots,
     reduce_here,
     adjacency,
-    halo,
+    halo_own,
+    halo_core,
+    halo_across,
+    halo_diagonal,
     meta,
     grad_own,
     grad_core,
@@ -288,7 +310,7 @@
     mine_wide = lax.axis_index("wide")
     mine, core, across, diagonal = partners(4)
     barrier = greet(peer_count, mine_wide, mine, core, across)
-    replicas = halo.shape[0]
+    replicas = meta.shape[0]
     node_rows, width = feats.shape
     halo_rows = peer_count * slots
     quarter = node_rows // replicas
@@ -297,10 +319,11 @@
     per_half = peer_count // 2
 
     table[:node_rows, :] = feats[...]
-    for r in range(replicas):
+    halos = ((mine, halo_own), (core, halo_core), (across, halo_across), (diagonal, halo_diagonal))
+    for r, halo in halos:
         for first in range(0, peer_count, 8):
-            start = node_rows + r * halo_rows + first * slots
-            table[start : start + 8 * slots, :] = unfolded(halo[r, first : first + 8])
+            start = pl.multiple_of(node_rows + r * halo_rows + first * slots, 8 * slots)
+            table[pl.ds(start, 8 * slots), :] = unfolded(halo[first : first + 8])
     eye = lax.broadcasted_iota(jnp.int32, (LANES, LANES), 0) == lax.broadcasted_iota(
         jnp.int32, (LANES, LANES), 1
     )
@@ -344,7 +367,7 @@
         start = owner_rep * share + lax.rem(owner_wide, per_half) * rows
         return weights.at[owner_wide // per_half, pl.ds(pl.multiple_of(start, rows), rows)]
 
-    part_copies, halo_copies, full_copies = [], [], []
+    part_copies, halo_copies = [], []
     if reduce_here:
         for step in range(1, peer_count):
             peer = lax.rem(mine_wide + step, peer_count)
@@ -394,15 +417,32 @@
             total = total + came_weight[step].astype(jnp.float32)
         summed[...] = total.astype(jnp.bfloat16)
         spot = place(mine_wide, mine)
-        for step in range(1, peer_count):
-            peer = lax.rem(mine_wide + step, peer_count)
-            full_copies.append(
-                push(summed, spot, full_send.at[step], full_recv.at[step], peer, mine)
-            )
-        across_copies = [
-            push(summed, spot, rep_send.at[0, 0], rep_recv.at[0, 0], mine_wide, across)
-        ]
-        core_copies = [push(summed, spot, rep_send.at[1, 0], rep_recv.at[1, 0], mine_wide, core)]
+        beside = mine_wide + 1 - 2 * lax.rem(mine_wide, 2)
+        hops = list(range(1, per_half))
+        full_copies = {}
+        across_copies, core_copies = {}, {}
+
+        def share_piece(slot, src, dst):
+            across_copies[slot] = push(
+                src, dst, rep_send.at[0, slot], rep_recv.at[0, slot], mine_wide, across
+            )
+            core_copies[slot] = push(
+                src, dst, rep_send.at[1, slot], rep_recv.at[1, slot], mine_wide, core
+            )
+
+        def owner_of(slot):
+            base = mine_wide if slot < per_half else beside
+            return lax.rem(base + peer_count - 2 * (slot % per_half), peer_count)
+
+        full_copies[per_half] = push(
+            summed, spot, full_send.at[per_half], full_recv.at[per_half], beside, mine
+        )
+        share_piece(0, summed, spot)
+        for hop in hops:
+            peer = lax.rem(mine_wide + 2 * hop, peer_count)
+            full_copies[hop] = push(
+                summed, spot, full_send.at[hop], full_recv.at[hop], peer, mine
+            )
         own_slice = pltpu.make_async_copy(summed, spot, local_sem.at[1])
         own_slice.start()
 
@@ -414,16 +454,17 @@
     back_core = push(block, block, back_send.at[1], back_recv.at[1], mine_wide, core)
 
     if reduce_here:
-        for step in range(1, peer_count):
-            full_copies[step - 1].wait_recv()
-            owner = lax.rem(mine_wide + peer_count - step, peer_count)
-            spot = place(owner, mine)
-            across_copies.append(
-                push(spot, spot, rep_send.at[0, step], rep_recv.at[0, step], mine_wide, across)
-            )
-            core_copies.append(
-                push(spot, spot, rep_send.at[1, step], rep_recv.at[1, step], mine_wide, core)
-            )
+        order = [per_half] + sorted(hops, key=lambda hop: min(hop, per_half - hop))
+        order = order + [per_half + hop for hop in order[1:]]
+        for slot in order:
+            full_copies[slot].wait_recv()
+            spot = place(owner_of(slot), mine)
+            if slot < per_half:
+                ahead = per_half + slot
+                full_copies[ahead] = push(
+                    spot, spot, full_send.at[ahead], full_recv.at[ahead], beside, mine
+                )
+            share_piece(slot, spot, spot)
 
     back_across.wait_recv()
     block = came_halo.at[across]
@@ -442,20 +483,35 @@
 
     if reduce_here:
         onward = []
-        for step in range(peer_count):
-            across_copies[step].wait_recv()
-            owner = lax.rem(mine_wide + peer_count - step, peer_count)
-            spot = place(owner, across)
+        for slot in [0] + order:
+            across_copies[slot].wait_recv()
+            spot = place(owner_of(slot), across)
             onward.append(
-                push(spot, spot, rep_send.at[2, step], rep_recv.at[2, step], mine_wide, core)
-            )
-        for copy in core_copies + onward:
+                push(spot, spot, rep_send.at[2, slot], rep_recv.at[2, slot], mine_wide, core)
+            )
+        sent = list(full_copies.values()) + list(across_copies.values())
+        sent = sent + list(core_copies.values()) + onward
+        for copy in list(core_copies.values()) + onward:
             copy.wait_recv()
-        for copy in part_copies + full_copies + across_copies + core_copies + onward:
+        for copy in part_copies + sent:
             copy.wait_send()
         own_slice.wait()
     for copy in halo_copies + [back_across, back_core, back_onward]:
         copy.wait_send()
+
+
+def deliver(out_feats, grad_feats, weights, out_to, grad_to, self_to, neigh_to, sems):
+    pairs = (
+        (out_feats, out_to),
+        (grad_feats, grad_to),
+        (weights.at[0], self_to),
+        (weights.at[1], neigh_to),
+    )
+    copies = [pltpu.make_async_copy(src, dst, sems.at[n]) for n, (src, dst) in enumerate(pairs)]
+    for copy in copies:
+        copy.start()
+    for copy in copies:
+        copy.wait()
 
 
 def on_device(
@@ -489,12 +545,12 @@
     halo_shape = (replicas, peer_count, 2 * slots, width // 2)
     meta_shape = (8 + peer_count, tile_total)
     with jax.named_scope("spread_inputs"):
-        all_bits, all_meta, all_halo = pl.pallas_call(
+        all_bits, all_meta, halo = pl.pallas_call(
             functools.partial(spread_inputs, peer_count, slots),
             out_shape=(
                 shaped((replicas,) + words.shape, jnp.int32),
                 shaped((replicas,) + meta_shape, jnp.int32),
-                shaped(halo_shape, jnp.bfloat16),
+                shaped(halo_shape[1:], jnp.bfloat16),
             ),
             in_specs=[vmem_spec] * 5,
             out_specs=(any_spec,) * 3,
@@ -513,9 +569,13 @@
             ),
         )(words, tile_dst[0], tile_src[0], send_rows[0], node_feats)
 
+    halo_across = lax.ppermute(halo, "rep", by_chip)
+    halo_core = lax.ppermute(halo, "rep", by_core)
+    halo_diagonal = lax.ppermute(halo_across, "rep", by_core)
+
     columns = node_rows + replicas * halo_rows
-    pair_count = columns // LANES
     dst_count = node_rows // BLOCK
+    sum_shape = (dst_count * (dst_count + replicas // 2 * halo_blocks) // 2, BLOCK, LANES)
     with jax.named_scope("build_adjacency"):
         adjacency = pl.pallas_call(
             functools.partial(build_adjacency, dst_count, halo_blocks),
@@ -523,8 +583,11 @@
             in_specs=[smem_spec, vmem_spec],
             out_specs=vmem_spec,
             scratch_shapes=[
-                pltpu.VMEM((dst_count * pair_count, BLOCK, LANES), jnp.float32),
+                pltpu.VMEM(sum_shape, jnp.bfloat16),
+                pltpu.VMEM(sum_shape, jnp.bfloat16),
                 pltpu.VMEM((replicas * words.shape[0], 2 * LANES), jnp.bfloat16),
+                pltpu.VMEM((replicas * words.shape[0], 2 * LANES), jnp.float32),
+                pltpu.VMEM((replicas * words.shape[0], 2 * LANES), jnp.float32),
             ],
             compiler_params=pltpu.CompilerParams(vmem_limit_bytes=VMEM_BYTES),
             cost_estimate=pl.CostEstimate(
@@ -544,7 +607,7 @@
                 shaped((2, width, width), jnp.bfloat16),
                 shaped((2 * width // replicas, width), jnp.bfloat16),
             ),
-            in_specs=[vmem_spec] * 11,
+            in_specs=[vmem_spec] * 14,
             out_specs=(vmem_spec, vmem_spec, any_spec, vmem_spec),
             scratch_shapes=[
                 pltpu.VMEM((columns, width), jnp.bfloat16),
@@ -567,7 +630,10 @@
             ),
         )(
             adjacency,
-            all_halo,
+            halo,
+            halo_core,
+            halo_across,
+            halo_diagonal,
             all_meta,
             grad_out,
             grad_core,
@@ -579,7 +645,19 @@
             norm_count.reshape(-1, LANES),
         )
     if reduce_here:
-        return out_feats, grad_feats, weights[0], weights[1]
+        with jax.named_scope("deliver"):
+            return pl.pallas_call(
+                deliver,
+                out_shape=(
+                    shaped((quarter, width), jnp.bfloat16),
+                    shaped((quarter, width), jnp.bfloat16),
+                    shaped((width, width), jnp.bfloat16),
+                    shaped((width, width), jnp.bfloat16),
+                ),
+                in_specs=[vmem_spec] * 3,
+                out_specs=(any_spec,) * 4,
+                scratch_shapes=[dma(4)],
+            )(out_feats, grad_feats, weights)
     total = lax.psum(weight_grad.astype(jnp.float32), "wide").astype(jnp.bfloat16)
     whole = lax.all_gather(total, "rep", axis=0, tiled=False)
     share = width // replicas

time: 65.4 us -> 65.9 us (level)
  local copies, waits for them, and re-layouts: 5.42 us -> 0.78 us
  waiting for transfers between devices: 0.01 us -> 2.38 us
  starting transfers between devices: 3.44 us -> 5.79 us
    pallas_call x1, Pallas kernels: 13.8 us -> 11.3 us  [on_device(): pl.pallas_call(functools.partial(spread_inputs, peer_count, slots), out_s...]
    pallas_call x0 -> x1, Pallas kernels: none -> 2.57 us  [on_device(): pl.pallas_call(deliver, out_shape=(shaped((quarter, width), jnp.bfloat16)...]
    unnamed x10 -> x12, local copies, waits for them, and re-layouts: 3.15 us -> 0.78 us
    ppermute x0 -> x3, waiting for transfers between devices: none -> 2.37 us  [the longest x1 2.36 us: on_device(): halo_across = lax.ppermute(halo, 'rep', by_chip)]
    squeeze x1 -> x0, local copies, waits for them, and re-layouts: 2.28 us -> none  [on_device(): return (out_feats, grad_feats, weights[0], weights[1])]
    ppermute x0 -> x3, starting transfers between devices: none -> 2.21 us  [the longest x1 1.78 us: on_device(): halo_across = lax.ppermute(halo, 'rep', by_chip)]
    pallas_call x1, Pallas kernels: 31.2 us -> 32.9 us  [on_device(): pl.pallas_call(functools.partial(layer, peer_count, slots, reduce_here),...]
    pallas_call x1, Pallas kernels: 10.5 us -> 9.32 us  [on_device(): pl.pallas_call(functools.partial(build_adjacency, dst_count, halo_blocks)...]
  transfers between devices with their start and end apart: 3 -> 6, of which waited for: 0 -> 1; matrix products, arithmetic and copies ran while one was open for 0% -> 0% of each run, Pallas kernels for 37% -> 31%
where the time goes in v3:
time: 65.9 us; the launch traced here: 65.7 us
  Pallas kernels  56.1 us (85%)
  starting transfers between devices  5.79 us (9%)
  waiting for transfers between devices  2.38 us (4%)
  local copies, waits for them, and re-layouts  0.78 us (1%)
  between operations  0.73 us (1%)
    pallas_call x1, Pallas kernels, on_device(): pl.pallas_call(functools.partial(layer, peer_count, slots, reduce_here),...  32.9 us
    pallas_call x1, Pallas kernels, on_device(): pl.pallas_call(functools.partial(spread_inputs, peer_count, slots), out_s...  11.3 us
    pallas_call x1, Pallas kernels, on_device(): pl.pallas_call(functools.partial(build_adjacency, dst_count, halo_blocks)...  9.32 us
    ppermute x1, starting transfers between devices, on_device(): grad_across = lax.ppermute(grad_out, 'rep', by_chip)  3 us
    pallas_call x1, Pallas kernels, on_device(): pl.pallas_call(deliver, out_shape=(shaped((quarter, width), jnp.bfloat16)...  2.57 us
    ppermute x1, waiting for transfers between devices, on_device(): halo_across = lax.ppermute(halo, 'rep', by_chip)  2.36 us
    ppermute x1, starting transfers between devices, on_device(): halo_across = lax.ppermute(halo, 'rep', by_chip)  1.78 us
  transfers between devices with their start and end apart: 6, of which 1 were waited for; matrix products, arithmetic and copies ran while one was open for 0% of the time, Pallas kernels for 31%

profile of v3, /device:TPU:0, one launch (start us, length us, event | category | flops | bytes accessed | tf_op | source)
XLA Modules:
  0.0 65.7 jit_solution(15782096309365120866)
XLA Ops:
  0.6 3.0 %collective-permute-start.4 = (bf16[256,512]{1,0:T(8,128)(2,1)}, bf16[256,512]{1,0:T(8,128)(2,1)S(1)}, u32[]{:S(2)}, u32[]{:S(2)}) collective-permute-start(bf16[256,512]{1,0:T(8,128)(2,1)} %grad_own.1), channel_id=1, source_target_pairs={{0,2},{1,3},{2,0},{3,1},{4,6},{5,7},{6,4},{7,5},{8,10},{9,11},{10,... | collective-permute-start | bytes 786440 | tf_op jit(solution)/shard_map/ppermute | solution.py:541
  3.6 11.3 %spread_inputs.1 = (s32[4,256,128]{2,1,0:T(8,128)}, s32[4,16,128]{2,1,0:T(8,128)}, bf16[8,16,256]{2,1,0:T(8,128)(2,1)}) custom-call(s32[256,128]{1,0:T(8,128)} %bitcast.5, s32[1,128]{1,0:T(1,128)} %bitcast.8, s32[1,128]{1,0:T(1,128)} %bitcast.9, s32[8,8]{1,0:T(8,128)} %bitcast.6, bf16[1024,512]{1,0:T(8,128)(2,1)} %feats.3), custom_call_target="tpu_custom_call" | custom-call | tf_op jit(solution)/shard_map/spread_inputs/pallas_call | solution.py:548
  14.9 1.8 %collective-permute-start.1 = (bf16[8,16,256]{2,1,0:T(8,128)(2,1)}, bf16[8,16,256]{2,1,0:T(8,128)(2,1)S(1)}, u32[]{:S(2)}, u32[]{:S(2)}) collective-permute-start(bf16[8,16,256]{2,1,0:T(8,128)(2,1)} %get-tuple-element.12.halo_own), channel_id=1, source_target_pairs={{0,2},{1,3},{2,0},{3,1},{4,6},{5,7},{6,4},{7,5},{8,10},{9,11},{10,... | collective-permute-start | bytes 196616 | tf_op jit(solution)/shard_map/ppermute | solution.py:572
  16.7 0.1 collective-permute-start.3
  16.8 0.4 collective-permute-start
  17.2 2.4 %collective-permute-done.1.halo_across = bf16[8,16,256]{2,1,0:T(8,128)(2,1)S(1)} collective-permute-done((bf16[8,16,256]{2,1,0:T(8,128)(2,1)}, bf16[8,16,256]{2,1,0:T(8,128)(2,1)S(1)}, u32[]{:S(2)}, u32[]{:S(2)}) %collective-permute-start.1) | collective-permute-done | bytes 65568 | tf_op jit(solution)/shard_map/ppermute | solution.py:572
  19.6 0.0 copy-start.3
  19.6 0.0 collective-permute-start.2
  19.6 0.0 collective-permute-done.4.grad_across
  19.6 0.0 copy-start
  19.6 0.5 collective-permute-start.5
  20.1 9.3 %build_adjacency.1.adjacency = bf16[1024,1280]{1,0:T(8,128)(2,1)} custom-call(s32[4,16,128]{2,1,0:T(8,128)} %get-tuple-element.10.meta, s32[4,256,128]{2,1,0:T(8,128)} %get-tuple-element.11.bits), custom_call_target="tpu_custom_call" | custom-call | flops 8000000000 | bytes 4000000 | tf_op jit(solution)/shard_map/build_adjacency/pallas_call | solution.py:580
  29.4 0.0 copy-done.3
  29.4 0.0 copy-done
  29.4 0.0 collective-permute-done.halo_core
  29.4 0.0 copy-start.4
  29.4 0.0 collective-permute-done.2.halo_diagonal
  29.4 0.0 copy-start.5
  29.4 0.0 collective-permute-done.3.grad_core
  29.4 0.0 copy-start.1
  29.5 0.0 collective-permute-done.5.grad_diagonal
  29.5 0.0 copy-start.2
  29.5 0.6 copy-done.4
  30.0 0.0 copy-done.5
  30.0 0.1 copy-done.1
  30.1 0.1 copy-done.2
  30.2 32.9 %layer.1 = (bf16[256,512]{1,0:T(8,128)(2,1)}, bf16[256,512]{1,0:T(8,128)(2,1)}, bf16[2,512,512]{2,1,0:T(8,128)(2,1)}, bf16[256,512]{1,0:T(8,128)(2,1)}) custom-call(bf16[1024,1280]{1,0:T(8,128)(2,1)} %build_adjacency.1.adjacency, bf16[8,16,256]{2,1,0:T(8,128)(2,1)} %get-tuple-element.12.halo_own, bf16[8,16,256]{2,1,0:T(8,128)(2,1)} %copy-done.4, ...), custom_call_target="tpu_custom_call" | custom-call | tf_op jit(solution)/shard_map/layer/pallas_call | solution.py:602
  63.2 2.6 %deliver.1 = (bf16[256,512]{1,0:T(8,128)(2,1)}, bf16[256,512]{1,0:T(8,128)(2,1)}, bf16[512,512]{1,0:T(8,128)(2,1)}, bf16[512,512]{1,0:T(8,128)(2,1)}) custom-call(bf16[256,512]{1,0:T(8,128)(2,1)} %get-tuple-element.13.out_feats, bf16[256,512]{1,0:T(8,128)(2,1)} %get-tuple-element.14.grad_feats, bf16[2,512,512]{2,1,0:T(8,128)(2,1)} %get-tuple-element.15.weights), custom_call_target="tpu_custom_call" | custom-call | tf_op jit(solution)/shard_map/deliver/pallas_call | solution.py:649
Async XLA Ops:
  0.6 18.9 %collective-permute-start.4 = (bf16[256,512]{1,0:T(8,128)(2,1)}, bf16[256,512]{1,0:T(8,128)(2,1)S(1)}, u32[]{:S(2)}, u32[]{:S(2)}) collective-permute-start(bf16[256,512]{1,0:T(8,128)(2,1)} %grad_own.1), channel_id=1, source_target_pairs={{0,2},{1,3},{2,0},{3,1},{4,6},{5,7},{6,4},{7,5},{8,10},{9,11},{10,... | collective-permute-start | bytes 786440 | tf_op jit(solution)/shard_map/ppermute | solution.py:541
  14.9 4.7 %collective-permute-start.1 = (bf16[8,16,256]{2,1,0:T(8,128)(2,1)}, bf16[8,16,256]{2,1,0:T(8,128)(2,1)S(1)}, u32[]{:S(2)}, u32[]{:S(2)}) collective-permute-start(bf16[8,16,256]{2,1,0:T(8,128)(2,1)} %get-tuple-element.12.halo_own), channel_id=1, source_target_pairs={{0,2},{1,3},{2,0},{3,1},{4,6},{5,7},{6,4},{7,5},{8,10},{9,11},{10,... | collective-permute-start | bytes 196616 | tf_op jit(solution)/shard_map/ppermute | solution.py:572
  16.7 12.8 %collective-permute-start.3 = (bf16[256,512]{1,0:T(8,128)(2,1)}, bf16[256,512]{1,0:T(8,128)(2,1)S(1)}, u32[]{:S(2)}, u32[]{:S(2)}) collective-permute-start(bf16[256,512]{1,0:T(8,128)(2,1)} %grad_own.1), channel_id=1, source_target_pairs={{0,1},{1,0},{2,3},{3,2},{4,5},{5,4},{6,7},{7,6},{8,9},{9,8},{10,11... | collective-permute-start | bytes 786440 | tf_op jit(solution)/shard_map/ppermute | solution.py:542
  16.8 12.6 %collective-permute-start = (bf16[8,16,256]{2,1,0:T(8,128)(2,1)}, bf16[8,16,256]{2,1,0:T(8,128)(2,1)S(1)}, u32[]{:S(2)}, u32[]{:S(2)}) collective-permute-start(bf16[8,16,256]{2,1,0:T(8,128)(2,1)} %get-tuple-element.12.halo_own), channel_id=1, source_target_pairs={{0,1},{1,0},{2,3},{3,2},{4,5},{5,4},{6,7},{7,6},{8,9},{9,8},{10,11... | collective-permute-start | bytes 196616 | tf_op jit(solution)/shard_map/ppermute | solution.py:573
  19.6 9.8 %copy-start.3 = (bf16[8,16,256]{2,1,0:T(8,128)(2,1)}, bf16[8,16,256]{2,1,0:T(8,128)(2,1)S(1)}, u32[]{:S(2)}) copy-start(bf16[8,16,256]{2,1,0:T(8,128)(2,1)S(1)} %collective-permute-done.1.halo_across) | copy-start | bytes 196612
  19.6 9.9 %collective-permute-start.2 = (bf16[8,16,256]{2,1,0:T(8,128)(2,1)S(1)}, bf16[8,16,256]{2,1,0:T(8,128)(2,1)S(1)}, u32[]{:S(2)}, u32[]{:S(2)}) collective-permute-start(bf16[8,16,256]{2,1,0:T(8,128)(2,1)S(1)} %collective-permute-done.1.halo_across), channel_id=1, source_target_pairs={{0,1},{1,0},{2,3},{3,2},{4,5},{5,4},{6,7},{7,6},{8,9},{9,8},{10,11... | collective-permute-start | bytes 196616 | tf_op jit(solution)/shard_map/ppermute | solution.py:574
  19.6 9.8 %copy-start = (bf16[256,512]{1,0:T(8,128)(2,1)}, bf16[256,512]{1,0:T(8,128)(2,1)S(1)}, u32[]{:S(2)}) copy-start(bf16[256,512]{1,0:T(8,128)(2,1)S(1)} %collective-permute-done.4.grad_across) | copy-start | bytes 786436
  19.6 9.9 %collective-permute-start.5 = (bf16[256,512]{1,0:T(8,128)(2,1)S(1)}, bf16[256,512]{1,0:T(8,128)(2,1)S(1)}, u32[]{:S(2)}, u32[]{:S(2)}) collective-permute-start(bf16[256,512]{1,0:T(8,128)(2,1)S(1)} %collective-permute-done.4.grad_across), channel_id=1, source_target_pairs={{0,1},{1,0},{2,3},{3,2},{4,5},{5,4},{6,7},{7,6},{8,9},{9,8},{10,11... | collective-permute-start | bytes 786440 | tf_op jit(solution)/shard_map/ppermute | solution.py:543
  29.4 0.6 copy-start.4
  29.4 0.6 copy-start.5
  29.4 0.7 %copy-start.1 = (bf16[256,512]{1,0:T(8,128)(2,1)}, bf16[256,512]{1,0:T(8,128)(2,1)S(1)}, u32[]{:S(2)}) copy-start(bf16[256,512]{1,0:T(8,128)(2,1)S(1)} %collective-permute-done.3.grad_core) | copy-start | bytes 786436
  29.5 0.8 %copy-start.2 = (bf16[256,512]{1,0:T(8,128)(2,1)}, bf16[256,512]{1,0:T(8,128)(2,1)S(1)}, u32[]{:S(2)}) copy-start(bf16[256,512]{1,0:T(8,128)(2,1)S(1)} %collective-permute-done.5.grad_diagonal) | copy-start | bytes 786436

commit v4 on v3

--- a/solution.py
+++ b/solution.py
@@ -112,7 +112,7 @@
     feats,
     all_bits,
     all_meta,
-    halo,
+    all_halo,
     bits,
     meta,
     outgoing,
@@ -149,7 +149,7 @@
         exchange.append(
             push(
                 outgoing.at[peer],
-                halo.at[mine_wide],
+                all_halo.at[mine, mine_wide],
                 halo_send.at[step],
                 halo_recv.at[step],
                 peer,
@@ -169,17 +169,23 @@
         pltpu.make_async_copy(src, dst.at[mine], local_sem.at[n])
         for n, (src, dst) in enumerate(pairs)
     ]
-    own.append(
-        pltpu.make_async_copy(outgoing.at[mine_wide], halo.at[mine_wide], local_sem.at[2])
-    )
-    for copy in own:
+    kept = pltpu.make_async_copy(
+        outgoing.at[mine_wide], all_halo.at[mine, mine_wide], local_sem.at[2]
+    )
+    for copy in own + [kept]:
         copy.start()
+    kept.wait()
+    for copy in exchange:
+        copy.wait_recv()
+    block = all_halo.at[mine]
+    to_across.append(push(block, block, send_sem.at[2], recv_sem.at[2], mine_wide, across))
+    to_core.append(push(block, block, send_sem.at[5], recv_sem.at[5], mine_wide, core))
     onward = []
-    for n, dst in enumerate((all_bits, all_meta)):
+    for n, dst in enumerate((all_bits, all_meta, all_halo)):
         to_across[n].wait_recv()
         block = dst.at[across]
         onward.append(push(block, block, send_sem.at[6 + n], recv_sem.at[6 + n], mine_wide, core))
-    for copy in to_core + onward + exchange:
+    for copy in to_core + onward:
         copy.wait_recv()
     for copy in to_across + to_core + onward + exchange:
         copy.wait_send()
@@ -213,7 +219,7 @@
     factor = (1 << (7 - (bit & 7))).astype(jnp.float32) * (1.0 / 128.0)
     pattern = jnp.where(match, factor, 0.0)
     behind = (row & (GROUP - 1)) - (col >> 7)
-    lane_half = lax.broadcasted_iota(jnp.int32, (BLOCK, LANES), 1) >> 6
+    lane_half = lax.broadcasted_iota(jnp.int32, (1, LANES), 1) >> 6
 
     def expand(n):
         chosen = jnp.where(behind == 2 * n, pattern, 0.0).astype(jnp.bfloat16)
@@ -267,11 +273,8 @@
     peer_count,
     slots,
     reduce_here,
-    adjacency,
-    halo_own,
-    halo_core,
-    halo_across,
-    halo_diagonal,
+    adjacency_from,
+    halo,
     meta,
     grad_own,
     grad_core,
@@ -285,6 +288,7 @@
     grad_feats,
     weights,
     weight_grad,
+    adjacency,
     table,
     scale,
     agg,
@@ -306,6 +310,7 @@
     rep_recv,
     back_send,
     back_recv,
+    fetch_sem,
 ):
     mine_wide = lax.axis_index("wide")
     mine, core, across, diagonal = partners(4)
@@ -318,12 +323,22 @@
     rows = 2 * share // peer_count
     per_half = peer_count // 2
 
+    def rows_of(q):
+        return pl.ds(pl.multiple_of(q * quarter, quarter), quarter)
+
+    fetches = [
+        pltpu.make_async_copy(
+            adjacency_from.at[rows_of(q)], adjacency.at[rows_of(q)], fetch_sem.at[n]
+        )
+        for n, q in enumerate((mine, core, across, diagonal))
+    ]
+    for copy in fetches:
+        copy.start()
     table[:node_rows, :] = feats[...]
-    halos = ((mine, halo_own), (core, halo_core), (across, halo_across), (diagonal, halo_diagonal))
-    for r, halo in halos:
+    for r in range(replicas):
         for first in range(0, peer_count, 8):
-            start = pl.multiple_of(node_rows + r * halo_rows + first * slots, 8 * slots)
-            table[pl.ds(start, 8 * slots), :] = unfolded(halo[first : first + 8])
+            start = node_rows + r * halo_rows + first * slots
+            table[start : start + 8 * slots, :] = unfolded(halo[r, first : first + 8])
     eye = lax.broadcasted_iota(jnp.int32, (LANES, LANES), 0) == lax.broadcasted_iota(
         jnp.int32, (LANES, LANES), 1
     )
@@ -332,12 +347,10 @@
         column = jnp.sum(jnp.where(eye, counts, 0.0), axis=1, keepdims=True)
         scale[n * LANES : (n + 1) * LANES, :] = lax.rsqrt(column)
 
-    def rows_of(q):
-        return pl.ds(pl.multiple_of(q * quarter, quarter), quarter)
-
     parts = ((mine, grad_own), (core, grad_core), (across, grad_across), (diagonal, grad_diagonal))
-    for q, grad_out in parts:
+    for (q, grad_out), fetch in zip(parts, fetches):
         here = rows_of(q)
+        fetch.wait()
         sums = jnp.dot(adjacency[here, :], table[...], preferred_element_type=jnp.float32)
         part_scale = scale[here, :]
         part_agg = (sums * part_scale).astype(jnp.bfloat16)
@@ -545,15 +558,15 @@
     halo_shape = (replicas, peer_count, 2 * slots, width // 2)
     meta_shape = (8 + peer_count, tile_total)
     with jax.named_scope("spread_inputs"):
-        all_bits, all_meta, halo = pl.pallas_call(
+        all_bits, all_meta, all_halo = pl.pallas_call(
             functools.partial(spread_inputs, peer_count, slots),
             out_shape=(
                 shaped((replicas,) + words.shape, jnp.int32),
                 shaped((replicas,) + meta_shape, jnp.int32),
-                shaped(halo_shape[1:], jnp.bfloat16),
+                shaped(halo_shape, jnp.bfloat16),
             ),
             in_specs=[vmem_spec] * 5,
-            out_specs=(any_spec,) * 3,
+            out_specs=(vmem_spec,) * 3,
             scratch_shapes=[
                 pltpu.VMEM(words.shape, jnp.int32),
                 pltpu.VMEM(meta_shape, jnp.int32),
@@ -568,10 +581,6 @@
                 collective_id=0, has_side_effects=True, vmem_limit_bytes=VMEM_BYTES
             ),
         )(words, tile_dst[0], tile_src[0], send_rows[0], node_feats)
-
-    halo_across = lax.ppermute(halo, "rep", by_chip)
-    halo_core = lax.ppermute(halo, "rep", by_core)
-    halo_diagonal = lax.ppermute(halo_across, "rep", by_core)
 
     columns = node_rows + replicas * halo_rows
     dst_count = node_rows // BLOCK
@@ -607,9 +616,10 @@
                 shaped((2, width, width), jnp.bfloat16),
                 shaped((2 * width // replicas, width), jnp.bfloat16),
             ),
-            in_specs=[vmem_spec] * 14,
-            out_specs=(vmem_spec, vmem_spec, any_spec, vmem_spec),
+            in_specs=[any_spec] + [vmem_spec] * 10,
+            out_specs=(vmem_spec,) * 4,
             scratch_shapes=[
+                pltpu.VMEM((node_rows, columns), jnp.bfloat16),
                 pltpu.VMEM((columns, width), jnp.bfloat16),
                 pltpu.VMEM((node_rows, 1), jnp.float32),
                 pltpu.VMEM((node_rows, width), jnp.bfloat16),
@@ -624,16 +634,14 @@
             ]
             + [dma(peer_count)] * 6
             + [dma(3, peer_count)] * 2
-            + [dma(3)] * 2,
+            + [dma(3)] * 2
+            + [dma(replicas)],
             compiler_params=pltpu.CompilerParams(
                 collective_id=1, has_side_effects=True, vmem_limit_bytes=VMEM_BYTES
             ),
         )(
             adjacency,
-            halo,
-            halo_core,
-            halo_across,
-            halo_diagonal,
+            all_halo,
             all_meta,
             grad_out,
             grad_core,

time: 65.9 us -> 63.1 us (0.958)
  waiting for transfers between devices: 2.38 us -> 0.01 us
  starting transfers between devices: 5.79 us -> 3.44 us
  Pallas kernels: 56.1 us -> 58 us
    pallas_call x1, Pallas kernels: 11.3 us -> 14 us  [on_device(): pl.pallas_call(functools.partial(spread_inputs, peer_count, slots), out_s...]
    ppermute x3 -> x0, waiting for transfers between devices: 2.37 us -> none  [the longest x1 2.36 us: on_device(): halo_across = lax.ppermute(halo, 'rep', by_chip)]
    ppermute x3 -> x0, starting transfers between devices: 2.21 us -> none  [the longest x1 1.78 us: on_device(): halo_across = lax.ppermute(halo, 'rep', by_chip)]
    pallas_call x1, Pallas kernels: 32.9 us -> 32 us  [on_device(): pl.pallas_call(functools.partial(layer, peer_count, slots, reduce_here),...]
  transfers between devices with their start and end apart: 6 -> 3, of which waited for: 1 -> 0; matrix products, arithmetic and copies ran while one was open for 0% -> 0% of each run, Pallas kernels for 31% -> 37%
where the time goes in v4:
time: 63.1 us; the launch traced here: 62.9 us
  Pallas kernels  58 us (92%)
  starting transfers between devices  3.44 us (5%)
  local copies, waits for them, and re-layouts  0.77 us (1%)
  between operations  0.69 us (1%)
    pallas_call x1, Pallas kernels, on_device(): pl.pallas_call(functools.partial(layer, peer_count, slots, reduce_here),...  32 us
    pallas_call x1, Pallas kernels, on_device(): pl.pallas_call(functools.partial(spread_inputs, peer_count, slots), out_s...  14 us
    pallas_call x1, Pallas kernels, on_device(): pl.pallas_call(functools.partial(build_adjacency, dst_count, halo_blocks)...  9.32 us
    ppermute x1, starting transfers between devices, on_device(): grad_across = lax.ppermute(grad_out, 'rep', by_chip)  3 us
    pallas_call x1, Pallas kernels, on_device(): pl.pallas_call(deliver, out_shape=(shaped((quarter, width), jnp.bfloat16)...  2.57 us
  transfers between devices with their start and end apart: 3, of which 0 were waited for; matrix products, arithmetic and copies ran while one was open for 0% of the time, Pallas kernels for 37%

profile of v4, /device:TPU:0, one launch (start us, length us, event | category | flops | bytes accessed | tf_op | source)
XLA Modules:
  0.0 62.9 jit_solution(3020753753751572322)
XLA Ops:
  0.6 3.0 %collective-permute-start.1 = (bf16[256,512]{1,0:T(8,128)(2,1)}, bf16[256,512]{1,0:T(8,128)(2,1)S(1)}, u32[]{:S(2)}, u32[]{:S(2)}) collective-permute-start(bf16[256,512]{1,0:T(8,128)(2,1)} %grad_own.1), channel_id=1, source_target_pairs={{0,2},{1,3},{2,0},{3,1},{4,6},{5,7},{6,4},{7,5},{8,10},{9,11},{10,... | collective-permute-start | bytes 786440 | tf_op jit(solution)/shard_map/ppermute | solution.py:554
  3.6 0.0 collective-permute-start
  3.6 14.0 %spread_inputs.1 = (s32[4,256,128]{2,1,0:T(8,128)}, s32[4,16,128]{2,1,0:T(8,128)}, bf16[4,8,16,256]{3,2,1,0:T(8,128)(2,1)}) custom-call(s32[256,128]{1,0:T(8,128)} %bitcast.5, s32[1,128]{1,0:T(1,128)} %bitcast.8, s32[1,128]{1,0:T(1,128)} %bitcast.9, s32[8,8]{1,0:T(8,128)} %bitcast.6, bf16[1024,512]{1,0:T(8,128)(2,1)} %feats.3), custom_call_target="tpu_custom_call" | custom-call | tf_op jit(solution)/shard_map/spread_inputs/pallas_call | solution.py:561
  17.7 0.0 collective-permute-done.1.grad_across
  17.7 0.0 copy-start
  17.7 0.4 collective-permute-start.2
  18.1 9.3 %build_adjacency.1.adjacency_from = bf16[1024,1280]{1,0:T(8,128)(2,1)} custom-call(s32[4,16,128]{2,1,0:T(8,128)} %get-tuple-element.10.meta, s32[4,256,128]{2,1,0:T(8,128)} %get-tuple-element.11.bits), custom_call_target="tpu_custom_call" | custom-call | flops 8000000000 | bytes 4000000 | tf_op jit(solution)/shard_map/build_adjacency/pallas_call | solution.py:589
  27.5 0.0 copy-done
  27.5 0.0 collective-permute-done.grad_core
  27.5 0.0 copy-start.1
  27.5 0.0 collective-permute-done.2.grad_diagonal
  27.5 0.0 copy-start.2
  27.5 0.7 %copy-done.1 = bf16[256,512]{1,0:T(8,128)(2,1)} copy-done((bf16[256,512]{1,0:T(8,128)(2,1)}, bf16[256,512]{1,0:T(8,128)(2,1)S(1)}, u32[]{:S(2)}) %copy-start.1) | copy-done | bytes 262168
  28.2 0.1 copy-done.2
  28.3 32.0 %layer.1 = (bf16[256,512]{1,0:T(8,128)(2,1)}, bf16[256,512]{1,0:T(8,128)(2,1)}, bf16[2,512,512]{2,1,0:T(8,128)(2,1)}, bf16[256,512]{1,0:T(8,128)(2,1)}) custom-call(bf16[1024,1280]{1,0:T(8,128)(2,1)} %build_adjacency.1.adjacency_from, bf16[4,8,16,256]{3,2,1,0:T(8,128)(2,1)} %get-tuple-element.12.halo, s32[4,16,128]{2,1,0:T(8,128)} %get-tuple-element.10.meta, ...), custom_call_target="tpu_custom_call" | custom-call | tf_op jit(solution)/shard_map/layer/pallas_call | solution.py:611
  60.3 2.6 %deliver.1 = (bf16[256,512]{1,0:T(8,128)(2,1)}, bf16[256,512]{1,0:T(8,128)(2,1)}, bf16[512,512]{1,0:T(8,128)(2,1)}, bf16[512,512]{1,0:T(8,128)(2,1)}) custom-call(bf16[256,512]{1,0:T(8,128)(2,1)} %get-tuple-element.13.out_feats, bf16[256,512]{1,0:T(8,128)(2,1)} %get-tuple-element.14.grad_feats, bf16[2,512,512]{2,1,0:T(8,128)(2,1)} %get-tuple-element.15.weights), custom_call_target="tpu_custom_call" | custom-call | tf_op jit(solution)/shard_map/deliver/pallas_call | solution.py:657
Async XLA Ops:
  0.6 17.1 %collective-permute-start.1 = (bf16[256,512]{1,0:T(8,128)(2,1)}, bf16[256,512]{1,0:T(8,128)(2,1)S(1)}, u32[]{:S(2)}, u32[]{:S(2)}) collective-permute-start(bf16[256,512]{1,0:T(8,128)(2,1)} %grad_own.1), channel_id=1, source_target_pairs={{0,2},{1,3},{2,0},{3,1},{4,6},{5,7},{6,4},{7,5},{8,10},{9,11},{10,... | collective-permute-start | bytes 786440 | tf_op jit(solution)/shard_map/ppermute | solution.py:554
  3.6 23.8 %collective-permute-start = (bf16[256,512]{1,0:T(8,128)(2,1)}, bf16[256,512]{1,0:T(8,128)(2,1)S(1)}, u32[]{:S(2)}, u32[]{:S(2)}) collective-permute-start(bf16[256,512]{1,0:T(8,128)(2,1)} %grad_own.1), channel_id=1, source_target_pairs={{0,1},{1,0},{2,3},{3,2},{4,5},{5,4},{6,7},{7,6},{8,9},{9,8},{10,11... | collective-permute-start | bytes 786440 | tf_op jit(solution)/shard_map/ppermute | solution.py:555
  17.7 9.8 %copy-start = (bf16[256,512]{1,0:T(8,128)(2,1)}, bf16[256,512]{1,0:T(8,128)(2,1)S(1)}, u32[]{:S(2)}) copy-start(bf16[256,512]{1,0:T(8,128)(2,1)S(1)} %collective-permute-done.1.grad_across) | copy-start | bytes 786436
  17.7 9.8 %collective-permute-start.2 = (bf16[256,512]{1,0:T(8,128)(2,1)S(1)}, bf16[256,512]{1,0:T(8,128)(2,1)S(1)}, u32[]{:S(2)}, u32[]{:S(2)}) collective-permute-start(bf16[256,512]{1,0:T(8,128)(2,1)S(1)} %collective-permute-done.1.grad_across), channel_id=1, source_target_pairs={{0,1},{1,0},{2,3},{3,2},{4,5},{5,4},{6,7},{7,6},{8,9},{9,8},{10,11... | collective-permute-start | bytes 786440 | tf_op jit(solution)/shard_map/ppermute | solution.py:556
  27.5 0.7 %copy-start.1 = (bf16[256,512]{1,0:T(8,128)(2,1)}, bf16[256,512]{1,0:T(8,128)(2,1)S(1)}, u32[]{:S(2)}) copy-start(bf16[256,512]{1,0:T(8,128)(2,1)S(1)} %collective-permute-done.grad_core) | copy-start | bytes 786436
  27.5 0.8 %copy-start.2 = (bf16[256,512]{1,0:T(8,128)(2,1)}, bf16[256,512]{1,0:T(8,128)(2,1)S(1)}, u32[]{:S(2)}) copy-start(bf16[256,512]{1,0:T(8,128)(2,1)S(1)} %collective-permute-done.2.grad_diagonal) | copy-start | bytes 786436

commit v5 on v4

--- a/solution.py
+++ b/solution.py
@@ -277,9 +277,7 @@
     halo,
     meta,
     grad_own,
-    grad_core,
     grad_across,
-    grad_diagonal,
     feats,
     w_self,
     w_neigh,
@@ -288,6 +286,8 @@
     grad_feats,
     weights,
     weight_grad,
+    grad_core,
+    grad_diagonal,
     adjacency,
     table,
     scale,
@@ -311,6 +311,8 @@
     back_send,
     back_recv,
     fetch_sem,
+    out_send,
+    out_recv,
 ):
     mine_wide = lax.axis_index("wide")
     mine, core, across, diagonal = partners(4)
@@ -330,7 +332,7 @@
         pltpu.make_async_copy(
             adjacency_from.at[rows_of(q)], adjacency.at[rows_of(q)], fetch_sem.at[n]
         )
-        for n, q in enumerate((mine, core, across, diagonal))
+        for n, q in enumerate((mine, across, core, diagonal))
     ]
     for copy in fetches:
         copy.start()
@@ -347,10 +349,20 @@
         column = jnp.sum(jnp.where(eye, counts, 0.0), axis=1, keepdims=True)
         scale[n * LANES : (n + 1) * LANES, :] = lax.rsqrt(column)
 
-    parts = ((mine, grad_own), (core, grad_core), (across, grad_across), (diagonal, grad_diagonal))
-    for (q, grad_out), fetch in zip(parts, fetches):
+    pl.semaphore_wait(barrier, peer_count + 1)
+    to_core = push(grad_own, grad_core, out_send.at[0], out_recv.at[0], mine_wide, core)
+    onto_core = push(grad_across, grad_diagonal, out_send.at[1], out_recv.at[1], mine_wide, core)
+    parts = (
+        (mine, grad_own, None),
+        (across, grad_across, None),
+        (core, grad_core, to_core),
+        (diagonal, grad_diagonal, onto_core),
+    )
+    for (q, grad_out, arrival), fetch in zip(parts, fetches):
         here = rows_of(q)
         fetch.wait()
+        if arrival is not None:
+            arrival.wait()
         sums = jnp.dot(adjacency[here, :], table[...], preferred_element_type=jnp.float32)
         part_scale = scale[here, :]
         part_agg = (sums * part_scale).astype(jnp.bfloat16)
@@ -374,17 +386,23 @@
         jnp.bfloat16
     )
     weight_grad[share:, :] = transposed_times(agg[:, columns], grad_pre[...]).astype(jnp.bfloat16)
-    pl.semaphore_wait(barrier, peer_count + 1)
 
     def place(owner_wide, owner_rep):
-        start = owner_rep * share + lax.rem(owner_wide, per_half) * rows
-        return weights.at[owner_wide // per_half, pl.ds(pl.multiple_of(start, rows), rows)]
+        start = owner_rep * share + owner_wide // 2 * rows
+        return weights.at[lax.rem(owner_wide, 2), pl.ds(pl.multiple_of(start, rows), rows)]
+
+    def half_of(parity, owner_rep):
+        return weights.at[parity, pl.ds(pl.multiple_of(owner_rep * share, share), share)]
+
+    def slice_of(owner_wide):
+        start = (lax.rem(owner_wide, 2) * per_half + owner_wide // 2) * rows
+        return pl.ds(pl.multiple_of(start, rows), rows)
 
     part_copies, halo_copies = [], []
     if reduce_here:
         for step in range(1, peer_count):
             peer = lax.rem(mine_wide + step, peer_count)
-            piece = weight_grad.at[pl.ds(pl.multiple_of(peer * rows, rows), rows)]
+            piece = weight_grad.at[slice_of(peer)]
             part_copies.append(
                 push(
                     piece, came_weight.at[step], part_send.at[step], part_recv.at[step], peer, mine
@@ -422,42 +440,22 @@
     )
 
     if reduce_here:
-        total = weight_grad[pl.ds(pl.multiple_of(mine_wide * rows, rows), rows), :].astype(
-            jnp.float32
-        )
+        total = weight_grad[slice_of(mine_wide), :].astype(jnp.float32)
         for step in range(1, peer_count):
             part_copies[step - 1].wait_recv()
             total = total + came_weight[step].astype(jnp.float32)
         summed[...] = total.astype(jnp.bfloat16)
         spot = place(mine_wide, mine)
-        beside = mine_wide + 1 - 2 * lax.rem(mine_wide, 2)
-        hops = list(range(1, per_half))
-        full_copies = {}
-        across_copies, core_copies = {}, {}
-
-        def share_piece(slot, src, dst):
-            across_copies[slot] = push(
-                src, dst, rep_send.at[0, slot], rep_recv.at[0, slot], mine_wide, across
-            )
-            core_copies[slot] = push(
-                src, dst, rep_send.at[1, slot], rep_recv.at[1, slot], mine_wide, core
-            )
-
-        def owner_of(slot):
-            base = mine_wide if slot < per_half else beside
-            return lax.rem(base + peer_count - 2 * (slot % per_half), peer_count)
-
-        full_copies[per_half] = push(
-            summed, spot, full_send.at[per_half], full_recv.at[per_half], beside, mine
-        )
-        share_piece(0, summed, spot)
-        for hop in hops:
-            peer = lax.rem(mine_wide + 2 * hop, peer_count)
-            full_copies[hop] = push(
-                summed, spot, full_send.at[hop], full_recv.at[hop], peer, mine
-            )
+        parity = lax.rem(mine_wide, 2)
+        beside = mine_wide + 1 - 2 * parity
         own_slice = pltpu.make_async_copy(summed, spot, local_sem.at[1])
         own_slice.start()
+        full_copies = []
+        for hop in range(1, per_half):
+            peer = lax.rem(mine_wide + 2 * hop, peer_count)
+            full_copies.append(
+                push(summed, spot, full_send.at[hop], full_recv.at[hop], peer, mine)
+            )
 
     kept.wait()
     for copy in halo_copies:
@@ -467,17 +465,24 @@
     back_core = push(block, block, back_send.at[1], back_recv.at[1], mine_wide, core)
 
     if reduce_here:
-        order = [per_half] + sorted(hops, key=lambda hop: min(hop, per_half - hop))
-        order = order + [per_half + hop for hop in order[1:]]
-        for slot in order:
-            full_copies[slot].wait_recv()
-            spot = place(owner_of(slot), mine)
-            if slot < per_half:
-                ahead = per_half + slot
-                full_copies[ahead] = push(
-                    spot, spot, full_send.at[ahead], full_recv.at[ahead], beside, mine
-                )
-            share_piece(slot, spot, spot)
+        across_copies, core_copies = [], []
+
+        def share_half(n, block):
+            across_copies.append(
+                push(block, block, rep_send.at[0, n], rep_recv.at[0, n], mine_wide, across)
+            )
+            core_copies.append(
+                push(block, block, rep_send.at[1, n], rep_recv.at[1, n], mine_wide, core)
+            )
+
+        own_slice.wait()
+        for copy in full_copies:
+            copy.wait_recv()
+        block = half_of(parity, mine)
+        swap = push(block, block, full_send.at[0], full_recv.at[0], beside, mine)
+        share_half(0, block)
+        swap.wait_recv()
+        share_half(1, half_of(1 - parity, mine))
 
     back_across.wait_recv()
     block = came_halo.at[across]
@@ -496,19 +501,15 @@
 
     if reduce_here:
         onward = []
-        for slot in [0] + order:
-            across_copies[slot].wait_recv()
-            spot = place(owner_of(slot), across)
+        for n, block in enumerate((half_of(parity, across), half_of(1 - parity, across))):
+            across_copies[n].wait_recv()
             onward.append(
-                push(spot, spot, rep_send.at[2, slot], rep_recv.at[2, slot], mine_wide, core)
-            )
-        sent = list(full_copies.values()) + list(across_copies.values())
-        sent = sent + list(core_copies.values()) + onward
-        for copy in list(core_copies.values()) + onward:
+                push(block, block, rep_send.at[2, n], rep_recv.at[2, n], mine_wide, core)
+            )
+        for copy in core_copies + onward:
             copy.wait_recv()
-        for copy in part_copies + sent:
+        for copy in part_copies + full_copies + [swap] + across_copies + core_copies + onward:
             copy.wait_send()
-        own_slice.wait()
     for copy in halo_copies + [back_across, back_core, back_onward]:
         copy.wait_send()
 
@@ -548,12 +549,6 @@
 
     def dma(*dims):
         return pltpu.SemaphoreType.DMA(dims)
-
-    by_core = [(n, n + 1 - 2 * (n % 2)) for n in range(replicas)]
-    by_chip = [(n, (n + 2) % replicas) for n in range(replicas)]
-    grad_across = lax.ppermute(grad_out, "rep", by_chip)
-    grad_core = lax.ppermute(grad_out, "rep", by_core)
-    grad_diagonal = lax.ppermute(grad_across, "rep", by_core)
 
     halo_shape = (replicas, peer_count, 2 * slots, width // 2)
     meta_shape = (8 + peer_count, tile_total)
@@ -582,6 +577,10 @@
             ),
         )(words, tile_dst[0], tile_src[0], send_rows[0], node_feats)
 
+    grad_out, all_bits = lax.optimization_barrier((grad_out, all_bits))
+    by_chip = [(n, (n + 2) % replicas) for n in range(replicas)]
+    grad_across = lax.ppermute(grad_out, "rep", by_chip)
+
     columns = node_rows + replicas * halo_rows
     dst_count = node_rows // BLOCK
     sum_shape = (dst_count * (dst_count + replicas // 2 * halo_blocks) // 2, BLOCK, LANES)
@@ -616,9 +615,11 @@
                 shaped((2, width, width), jnp.bfloat16),
                 shaped((2 * width // replicas, width), jnp.bfloat16),
             ),
-            in_specs=[any_spec] + [vmem_spec] * 10,
+            in_specs=[any_spec] + [vmem_spec] * 8,
             out_specs=(vmem_spec,) * 4,
             scratch_shapes=[
+                pltpu.VMEM((quarter, width), jnp.bfloat16),
+                pltpu.VMEM((quarter, width), jnp.bfloat16),
                 pltpu.VMEM((node_rows, columns), jnp.bfloat16),
                 pltpu.VMEM((columns, width), jnp.bfloat16),
                 pltpu.VMEM((node_rows, 1), jnp.float32),
@@ -635,7 +636,8 @@
             + [dma(peer_count)] * 6
             + [dma(3, peer_count)] * 2
             + [dma(3)] * 2
-            + [dma(replicas)],
+            + [dma(replicas)]
+            + [dma(2)] * 2,
             compiler_params=pltpu.CompilerParams(
                 collective_id=1, has_side_effects=True, vmem_limit_bytes=VMEM_BYTES
             ),
@@ -644,9 +646,7 @@
             all_halo,
             all_meta,
             grad_out,
-            grad_core,
             grad_across,
-            grad_diagonal,
             node_feats,
             w_self,
             w_neigh,

time: 63.1 us -> 65.9 us (1.044)
  Pallas kernels: 58 us -> 63.1 us
  starting transfers between devices: 3.44 us -> 1.19 us
    pallas_call x1, Pallas kernels: 32 us -> 35.4 us  [on_device(): pl.pallas_call(functools.partial(layer, peer_count, slots, reduce_here),...]
    ppermute x1, starting transfers between devices: 3 us -> 1.19 us  [on_device(): grad_across = lax.ppermute(grad_out, 'rep', by_chip)]
    pallas_call x1, Pallas kernels: 14 us -> 15.8 us  [on_device(): pl.pallas_call(functools.partial(spread_inputs, peer_count, slots), out_s...]
  transfers between devices with their start and end apart: 3 -> 1, of which waited for: 0 -> 0; matrix products, arithmetic and copies ran while one was open for 0% -> 0% of each run, Pallas kernels for 37% -> 14%
where the time goes in v5:
time: 65.9 us; the launch traced here: 65.6 us
  Pallas kernels  63.1 us (96%)
  starting transfers between devices  1.19 us (2%)
  local copies, waits for them, and re-layouts  0.7 us (1%)
    pallas_call x1, Pallas kernels, on_device(): pl.pallas_call(functools.partial(layer, peer_count, slots, reduce_here),...  35.4 us
    pallas_call x1, Pallas kernels, on_device(): pl.pallas_call(functools.partial(spread_inputs, peer_count, slots), out_s...  15.8 us
    pallas_call x1, Pallas kernels, on_device(): pl.pallas_call(functools.partial(build_adjacency, dst_count, halo_blocks)...  9.3 us
    pallas_call x1, Pallas kernels, on_device(): pl.pallas_call(deliver, out_shape=(shaped((quarter, width), jnp.bfloat16)...  2.57 us
  transfers between devices with their start and end apart: 1, of which 0 were waited for; matrix products, arithmetic and copies ran while one was open for 0% of the time, Pallas kernels for 14%

profile of v5, /device:TPU:0, one launch (start us, length us, event | category | flops | bytes accessed | tf_op | source)
XLA Modules:
  0.0 65.6 jit_solution(4331417322021541860)
XLA Ops:
  0.6 15.8 %spread_inputs.1 = (s32[4,256,128]{2,1,0:T(8,128)}, s32[4,16,128]{2,1,0:T(8,128)}, bf16[4,8,16,256]{3,2,1,0:T(8,128)(2,1)}) custom-call(s32[256,128]{1,0:T(8,128)} %bitcast.5, s32[1,128]{1,0:T(1,128)} %bitcast.8, s32[1,128]{1,0:T(1,128)} %bitcast.9, s32[8,8]{1,0:T(8,128)} %bitcast.6, bf16[1024,512]{1,0:T(8,128)(2,1)} %feats.3), custom_call_target="tpu_custom_call" | custom-call | tf_op jit(solution)/shard_map/spread_inputs/pallas_call | solution.py:556
  16.4 1.2 %collective-permute-start = (bf16[256,512]{1,0:T(8,128)(2,1)}, bf16[256,512]{1,0:T(8,128)(2,1)S(1)}, u32[]{:S(2)}, u32[]{:S(2)}) collective-permute-start(bf16[256,512]{1,0:T(8,128)(2,1)} %grad_own), channel_id=1, source_target_pairs={{0,2},{1,3},{2,0},{3,1},{4,6},{5,7},{6,4},{7,5},{8,10},{9,11},{10,... | collective-permute-start | bytes 786440 | tf_op jit(solution)/shard_map/ppermute | solution.py:582
  17.6 9.3 %build_adjacency.1.adjacency_from = bf16[1024,1280]{1,0:T(8,128)(2,1)} custom-call(s32[4,16,128]{2,1,0:T(8,128)} %get-tuple-element.12.meta, s32[4,256,128]{2,1,0:T(8,128)} %get-tuple-element.14.bits), custom_call_target="tpu_custom_call" | custom-call | flops 8000000000 | bytes 4000000 | tf_op jit(solution)/shard_map/build_adjacency/pallas_call | solution.py:588
  26.9 0.0 collective-permute-done.grad_across
  26.9 0.0 copy-start
  26.9 0.7 %copy-done = bf16[256,512]{1,0:T(8,128)(2,1)} copy-done((bf16[256,512]{1,0:T(8,128)(2,1)}, bf16[256,512]{1,0:T(8,128)(2,1)S(1)}, u32[]{:S(2)}) %copy-start) | copy-done | bytes 262168
  27.6 35.4 %layer.1 = (bf16[256,512]{1,0:T(8,128)(2,1)}, bf16[256,512]{1,0:T(8,128)(2,1)}, bf16[2,512,512]{2,1,0:T(8,128)(2,1)}, bf16[256,512]{1,0:T(8,128)(2,1)}) custom-call(bf16[1024,1280]{1,0:T(8,128)(2,1)} %build_adjacency.1.adjacency_from, bf16[4,8,16,256]{3,2,1,0:T(8,128)(2,1)} %get-tuple-element.15.halo, s32[4,16,128]{2,1,0:T(8,128)} %get-tuple-element.12.meta, ...), custom_call_target="tpu_custom_call" | custom-call | tf_op jit(solution)/shard_map/layer/pallas_call | solution.py:610
  63.1 2.6 %deliver.1 = (bf16[256,512]{1,0:T(8,128)(2,1)}, bf16[256,512]{1,0:T(8,128)(2,1)}, bf16[512,512]{1,0:T(8,128)(2,1)}, bf16[512,512]{1,0:T(8,128)(2,1)}) custom-call(bf16[256,512]{1,0:T(8,128)(2,1)} %get-tuple-element.17.out_feats, bf16[256,512]{1,0:T(8,128)(2,1)} %get-tuple-element.18.grad_feats, bf16[2,512,512]{2,1,0:T(8,128)(2,1)} %get-tuple-element.19.weights), custom_call_target="tpu_custom_call" | custom-call | tf_op jit(solution)/shard_map/deliver/pallas_call | solution.py:657
Async XLA Ops:
  16.4 10.5 %collective-permute-start = (bf16[256,512]{1,0:T(8,128)(2,1)}, bf16[256,512]{1,0:T(8,128)(2,1)S(1)}, u32[]{:S(2)}, u32[]{:S(2)}) collective-permute-start(bf16[256,512]{1,0:T(8,128)(2,1)} %grad_own), channel_id=1, source_target_pairs={{0,2},{1,3},{2,0},{3,1},{4,6},{5,7},{6,4},{7,5},{8,10},{9,11},{10,... | collective-permute-start | bytes 786440 | tf_op jit(solution)/shard_map/ppermute | solution.py:582
  26.9 0.7 %copy-start = (bf16[256,512]{1,0:T(8,128)(2,1)}, bf16[256,512]{1,0:T(8,128)(2,1)S(1)}, u32[]{:S(2)}) copy-start(bf16[256,512]{1,0:T(8,128)(2,1)S(1)} %collective-permute-done.grad_across) | copy-start | bytes 786436

commit v6 on v4

--- a/solution.py
+++ b/solution.py
@@ -129,33 +129,9 @@
     meta[0:1, :] = tile_dst[...]
     meta[1:2, :] = tile_src[...]
     meta[8:, :slots] = send_rows[...]
-    node_rows = feats.shape[0]
-    for first in range(0, peer_count, 8):
-        picks = as_column(send_rows[first : first + 8, :])
-        chosen = picks == lax.broadcasted_iota(jnp.int32, (8 * slots, node_rows), 1)
-        rows = jnp.dot(
-            jnp.where(chosen, 1.0, 0.0).astype(jnp.bfloat16),
-            feats[...],
-            preferred_element_type=jnp.float32,
-        )
-        for n in range(8):
-            outgoing[first + n] = folded(rows[n * slots : (n + 1) * slots])
     sort_words(words, bits)
     pl.semaphore_wait(barrier, peer_count + 1)
 
-    exchange = []
-    for step in range(1, peer_count):
-        peer = lax.rem(mine_wide + step, peer_count)
-        exchange.append(
-            push(
-                outgoing.at[peer],
-                all_halo.at[mine, mine_wide],
-                halo_send.at[step],
-                halo_recv.at[step],
-                peer,
-                mine,
-            )
-        )
     pairs = ((bits, all_bits), (meta, all_meta))
     to_across = [
         push(src, dst.at[mine], send_sem.at[n], recv_sem.at[n], mine_wide, across)
@@ -169,11 +145,36 @@
         pltpu.make_async_copy(src, dst.at[mine], local_sem.at[n])
         for n, (src, dst) in enumerate(pairs)
     ]
+    for copy in own:
+        copy.start()
+    node_rows = feats.shape[0]
+    for first in range(0, peer_count, 8):
+        picks = as_column(send_rows[first : first + 8, :])
+        chosen = picks == lax.broadcasted_iota(jnp.int32, (8 * slots, node_rows), 1)
+        rows = jnp.dot(
+            jnp.where(chosen, 1.0, 0.0).astype(jnp.bfloat16),
+            feats[...],
+            preferred_element_type=jnp.float32,
+        )
+        for n in range(8):
+            outgoing[first + n] = folded(rows[n * slots : (n + 1) * slots])
+    exchange = []
+    for step in range(1, peer_count):
+        peer = lax.rem(mine_wide + step, peer_count)
+        exchange.append(
+            push(
+                outgoing.at[peer],
+                all_halo.at[mine, mine_wide],
+                halo_send.at[step],
+                halo_recv.at[step],
+                peer,
+                mine,
+            )
+        )
     kept = pltpu.make_async_copy(
         outgoing.at[mine_wide], all_halo.at[mine, mine_wide], local_sem.at[2]
     )
-    for copy in own + [kept]:
-        copy.start()
+    kept.start()
     kept.wait()
     for copy in exchange:
         copy.wait_recv()
@@ -365,9 +366,6 @@
             jnp.bfloat16
         )
         grad_pre[here, :] = back
-        grad_agg[here, :] = (times_transposed(back, w_neigh[...]) * part_scale).astype(
-            jnp.bfloat16
-        )
 
     columns = pl.ds(pl.multiple_of(mine * share, share), share)
     weight_grad[:share, :] = transposed_times(feats[:, columns], grad_pre[...]).astype(
@@ -380,7 +378,7 @@
         start = owner_rep * share + lax.rem(owner_wide, per_half) * rows
         return weights.at[owner_wide // per_half, pl.ds(pl.multiple_of(start, rows), rows)]
 
-    part_copies, halo_copies = [], []
+    part_copies, halo_copies, full_copies = [], [], []
     if reduce_here:
         for step in range(1, peer_count):
             peer = lax.rem(mine_wide + step, peer_count)
@@ -391,6 +389,9 @@
                 )
             )
 
+    grad_agg[...] = (times_transposed(grad_pre[...], w_neigh[...]) * scale[...]).astype(
+        jnp.bfloat16
+    )
     block = min(replicas * halo_rows, 512)
     for first in range(0, replicas * halo_rows, block):
         start = node_rows + first
@@ -430,32 +431,15 @@
             total = total + came_weight[step].astype(jnp.float32)
         summed[...] = total.astype(jnp.bfloat16)
         spot = place(mine_wide, mine)
-        beside = mine_wide + 1 - 2 * lax.rem(mine_wide, 2)
-        hops = list(range(1, per_half))
-        full_copies = {}
-        across_copies, core_copies = {}, {}
-
-        def share_piece(slot, src, dst):
-            across_copies[slot] = push(
-                src, dst, rep_send.at[0, slot], rep_recv.at[0, slot], mine_wide, across
-            )
-            core_copies[slot] = push(
-                src, dst, rep_send.at[1, slot], rep_recv.at[1, slot], mine_wide, core
-            )
-
-        def owner_of(slot):
-            base = mine_wide if slot < per_half else beside
-            return lax.rem(base + peer_count - 2 * (slot % per_half), peer_count)
-
-        full_copies[per_half] = push(
-            summed, spot, full_send.at[per_half], full_recv.at[per_half], beside, mine
-        )
-        share_piece(0, summed, spot)
-        for hop in hops:
-            peer = lax.rem(mine_wide + 2 * hop, peer_count)
-            full_copies[hop] = push(
-                summed, spot, full_send.at[hop], full_recv.at[hop], peer, mine
-            )
+        for step in range(1, peer_count):
+            peer = lax.rem(mine_wide + step, peer_count)
+            full_copies.append(
+                push(summed, spot, full_send.at[step], full_recv.at[step], peer, mine)
+            )
+        across_copies = [
+            push(summed, spot, rep_send.at[0, 0], rep_recv.at[0, 0], mine_wide, across)
+        ]
+        core_copies = [push(summed, spot, rep_send.at[1, 0], rep_recv.at[1, 0], mine_wide, core)]
         own_slice = pltpu.make_async_copy(summed, spot, local_sem.at[1])
         own_slice.start()
 
@@ -467,17 +451,16 @@
     back_core = push(block, block, back_send.at[1], back_recv.at[1], mine_wide, core)
 
     if reduce_here:
-        order = [per_half] + sorted(hops, key=lambda hop: min(hop, per_half - hop))
-        order = order + [per_half + hop for hop in order[1:]]
-        for slot in order:
-            full_copies[slot].wait_recv()
-            spot = place(owner_of(slot), mine)
-            if slot < per_half:
-                ahead = per_half + slot
-                full_copies[ahead] = push(
-                    spot, spot, full_send.at[ahead], full_recv.at[ahead], beside, mine
-                )
-            share_piece(slot, spot, spot)
+        for step in range(1, peer_count):
+            full_copies[step - 1].wait_recv()
+            owner = lax.rem(mine_wide + peer_count - step, peer_count)
+            spot = place(owner, mine)
+            across_copies.append(
+                push(spot, spot, rep_send.at[0, step], rep_recv.at[0, step], mine_wide, across)
+            )
+            core_copies.append(
+                push(spot, spot, rep_send.at[1, step], rep_recv.at[1, step], mine_wide, core)
+            )
 
     back_across.wait_recv()
     block = came_halo.at[across]
@@ -496,17 +479,16 @@
 
     if reduce_here:
         onward = []
-        for slot in [0] + order:
-            across_copies[slot].wait_recv()
-            spot = place(owner_of(slot), across)
+        for step in range(peer_count):
+            across_copies[step].wait_recv()
+            owner = lax.rem(mine_wide + peer_count - step, peer_count)
+            spot = place(owner, across)
             onward.append(
-                push(spot, spot, rep_send.at[2, slot], rep_recv.at[2, slot], mine_wide, core)
-            )
-        sent = list(full_copies.values()) + list(across_copies.values())
-        sent = sent + list(core_copies.values()) + onward
-        for copy in list(core_copies.values()) + onward:
+                push(spot, spot, rep_send.at[2, step], rep_recv.at[2, step], mine_wide, core)
+            )
+        for copy in core_copies + onward:
             copy.wait_recv()
-        for copy in part_copies + sent:
+        for copy in part_copies + full_copies + across_copies + core_copies + onward:
             copy.wait_send()
         own_slice.wait()
     for copy in halo_copies + [back_across, back_core, back_onward]:

time: 63.1 us -> 62.5 us (level)
    pallas_call x1, Pallas kernels: 32 us -> 31 us  [on_device(): pl.pallas_call(functools.partial(layer, peer_count, slots, reduce_here),...]
  transfers between devices with their start and end apart: 3 -> 3, of which waited for: 0 -> 0; matrix products, arithmetic and copies ran while one was open for 0% -> 0% of each run, Pallas kernels for 37% -> 38%
where the time goes in v6:
time: 62.5 us; the launch traced here: 62.3 us
  Pallas kernels  57.4 us (92%)
  starting transfers between devices  3.44 us (6%)
  local copies, waits for them, and re-layouts  0.77 us (1%)
  between operations  0.69 us (1%)
    pallas_call x1, Pallas kernels, on_device(): pl.pallas_call(functools.partial(layer, peer_count, slots, reduce_here),...  31 us
    pallas_call x1, Pallas kernels, on_device(): pl.pallas_call(functools.partial(spread_inputs, peer_count, slots), out_s...  14.4 us
    pallas_call x1, Pallas kernels, on_device(): pl.pallas_call(functools.partial(build_adjacency, dst_count, halo_blocks)...  9.32 us
    ppermute x1, starting transfers between devices, on_device(): grad_across = lax.ppermute(grad_out, 'rep', by_chip)  3 us
    pallas_call x1, Pallas kernels, on_device(): pl.pallas_call(deliver, out_shape=(shaped((quarter, width), jnp.bfloat16)...  2.57 us
  transfers between devices with their start and end apart: 3, of which 0 were waited for; matrix products, arithmetic and copies ran while one was open for 0% of the time, Pallas kernels for 38%

profile of v6, /device:TPU:0, one launch (start us, length us, event | category | flops | bytes accessed | tf_op | source)
XLA Modules:
  0.0 62.3 jit_solution(8608146950785592845)
XLA Ops:
  0.6 3.0 %collective-permute-start.1 = (bf16[256,512]{1,0:T(8,128)(2,1)}, bf16[256,512]{1,0:T(8,128)(2,1)S(1)}, u32[]{:S(2)}, u32[]{:S(2)}) collective-permute-start(bf16[256,512]{1,0:T(8,128)(2,1)} %grad_own.1), channel_id=1, source_target_pairs={{0,2},{1,3},{2,0},{3,1},{4,6},{5,7},{6,4},{7,5},{8,10},{9,11},{10,... | collective-permute-start | bytes 786440 | tf_op jit(solution)/shard_map/ppermute | solution.py:536
  3.6 0.0 collective-permute-start
  3.6 14.4 %spread_inputs.1 = (s32[4,256,128]{2,1,0:T(8,128)}, s32[4,16,128]{2,1,0:T(8,128)}, bf16[4,8,16,256]{3,2,1,0:T(8,128)(2,1)}) custom-call(s32[256,128]{1,0:T(8,128)} %bitcast.5, s32[1,128]{1,0:T(1,128)} %bitcast.8, s32[1,128]{1,0:T(1,128)} %bitcast.9, s32[8,8]{1,0:T(8,128)} %bitcast.6, bf16[1024,512]{1,0:T(8,128)(2,1)} %feats.3), custom_call_target="tpu_custom_call" | custom-call | tf_op jit(solution)/shard_map/spread_inputs/pallas_call | solution.py:543
  18.1 0.0 collective-permute-done.1.grad_across
  18.1 0.0 copy-start
  18.1 0.4 collective-permute-start.2
  18.5 9.3 %build_adjacency.1.adjacency_from = bf16[1024,1280]{1,0:T(8,128)(2,1)} custom-call(s32[4,16,128]{2,1,0:T(8,128)} %get-tuple-element.10.meta, s32[4,256,128]{2,1,0:T(8,128)} %get-tuple-element.11.bits), custom_call_target="tpu_custom_call" | custom-call | flops 8000000000 | bytes 4000000 | tf_op jit(solution)/shard_map/build_adjacency/pallas_call | solution.py:571
  27.9 0.0 copy-done
  27.9 0.0 collective-permute-done.grad_core
  27.9 0.0 copy-start.1
  27.9 0.0 collective-permute-done.2.grad_diagonal
  27.9 0.0 copy-start.2
  27.9 0.7 %copy-done.1 = bf16[256,512]{1,0:T(8,128)(2,1)} copy-done((bf16[256,512]{1,0:T(8,128)(2,1)}, bf16[256,512]{1,0:T(8,128)(2,1)S(1)}, u32[]{:S(2)}) %copy-start.1) | copy-done | bytes 262168
  28.6 0.1 copy-done.2
  28.7 31.0 %layer.1 = (bf16[256,512]{1,0:T(8,128)(2,1)}, bf16[256,512]{1,0:T(8,128)(2,1)}, bf16[2,512,512]{2,1,0:T(8,128)(2,1)}, bf16[256,512]{1,0:T(8,128)(2,1)}) custom-call(bf16[1024,1280]{1,0:T(8,128)(2,1)} %build_adjacency.1.adjacency_from, bf16[4,8,16,256]{3,2,1,0:T(8,128)(2,1)} %get-tuple-element.12.halo, s32[4,16,128]{2,1,0:T(8,128)} %get-tuple-element.10.meta, ...), custom_call_target="tpu_custom_call" | custom-call | tf_op jit(solution)/shard_map/layer/pallas_call | solution.py:593
  59.7 2.6 %deliver.1 = (bf16[256,512]{1,0:T(8,128)(2,1)}, bf16[256,512]{1,0:T(8,128)(2,1)}, bf16[512,512]{1,0:T(8,128)(2,1)}, bf16[512,512]{1,0:T(8,128)(2,1)}) custom-call(bf16[256,512]{1,0:T(8,128)(2,1)} %get-tuple-element.13.out_feats, bf16[256,512]{1,0:T(8,128)(2,1)} %get-tuple-element.14.grad_feats, bf16[2,512,512]{2,1,0:T(8,128)(2,1)} %get-tuple-element.15.weights), custom_call_target="tpu_custom_call" | custom-call | tf_op jit(solution)/shard_map/deliver/pallas_call | solution.py:639
Async XLA Ops:
  0.6 17.5 %collective-permute-start.1 = (bf16[256,512]{1,0:T(8,128)(2,1)}, bf16[256,512]{1,0:T(8,128)(2,1)S(1)}, u32[]{:S(2)}, u32[]{:S(2)}) collective-permute-start(bf16[256,512]{1,0:T(8,128)(2,1)} %grad_own.1), channel_id=1, source_target_pairs={{0,2},{1,3},{2,0},{3,1},{4,6},{5,7},{6,4},{7,5},{8,10},{9,11},{10,... | collective-permute-start | bytes 786440 | tf_op jit(solution)/shard_map/ppermute | solution.py:536
  3.6 24.2 %collective-permute-start = (bf16[256,512]{1,0:T(8,128)(2,1)}, bf16[256,512]{1,0:T(8,128)(2,1)S(1)}, u32[]{:S(2)}, u32[]{:S(2)}) collective-permute-start(bf16[256,512]{1,0:T(8,128)(2,1)} %grad_own.1), channel_id=1, source_target_pairs={{0,1},{1,0},{2,3},{3,2},{4,5},{5,4},{6,7},{7,6},{8,9},{9,8},{10,11... | collective-permute-start | bytes 786440 | tf_op jit(solution)/shard_map/ppermute | solution.py:537
  18.1 9.8 %copy-start = (bf16[256,512]{1,0:T(8,128)(2,1)}, bf16[256,512]{1,0:T(8,128)(2,1)S(1)}, u32[]{:S(2)}) copy-start(bf16[256,512]{1,0:T(8,128)(2,1)S(1)} %collective-permute-done.1.grad_across) | copy-start | bytes 786436
  18.1 9.8 %collective-permute-start.2 = (bf16[256,512]{1,0:T(8,128)(2,1)S(1)}, bf16[256,512]{1,0:T(8,128)(2,1)S(1)}, u32[]{:S(2)}, u32[]{:S(2)}) collective-permute-start(bf16[256,512]{1,0:T(8,128)(2,1)S(1)} %collective-permute-done.1.grad_across), channel_id=1, source_target_pairs={{0,1},{1,0},{2,3},{3,2},{4,5},{5,4},{6,7},{7,6},{8,9},{9,8},{10,11... | collective-permute-start | bytes 786440 | tf_op jit(solution)/shard_map/ppermute | solution.py:538
  27.9 0.7 %copy-start.1 = (bf16[256,512]{1,0:T(8,128)(2,1)}, bf16[256,512]{1,0:T(8,128)(2,1)S(1)}, u32[]{:S(2)}) copy-start(bf16[256,512]{1,0:T(8,128)(2,1)S(1)} %collective-permute-done.grad_core) | copy-start | bytes 786436
  27.9 0.8 %copy-start.2 = (bf16[256,512]{1,0:T(8,128)(2,1)}, bf16[256,512]{1,0:T(8,128)(2,1)S(1)}, u32[]{:S(2)}) copy-start(bf16[256,512]{1,0:T(8,128)(2,1)S(1)} %collective-permute-done.2.grad_diagonal) | copy-start | bytes 786436

commit v7 on v6

--- a/solution.py
+++ b/solution.py
@@ -417,11 +417,6 @@
         halo_out.at[mine_wide], came_halo.at[mine, mine_wide], local_sem.at[0]
     )
     kept.start()
-    own_rows = rows_of(mine)
-    total_grad = transposed_times(adjacency[:, own_rows], grad_agg[...]) + times_transposed(
-        grad_pre[own_rows, :], w_self[...]
-    )
-
     if reduce_here:
         total = weight_grad[pl.ds(pl.multiple_of(mine_wide * rows, rows), rows), :].astype(
             jnp.float32
@@ -461,6 +456,11 @@
             core_copies.append(
                 push(spot, spot, rep_send.at[1, step], rep_recv.at[1, step], mine_wide, core)
             )
+
+    own_rows = rows_of(mine)
+    total_grad = transposed_times(adjacency[:, own_rows], grad_agg[...]) + times_transposed(
+        grad_pre[own_rows, :], w_self[...]
+    )
 
     back_across.wait_recv()
     block = came_halo.at[across]

time: 62.5 us -> 62.5 us (level)
  no operation moved by 1% of the time
where the time goes in v7:
time: 62.5 us; the launch traced here: 62.3 us
  Pallas kernels  57.4 us (92%)
  starting transfers between devices  3.44 us (6%)
  local copies, waits for them, and re-layouts  0.77 us (1%)
  between operations  0.69 us (1%)
    pallas_call x1, Pallas kernels, on_device(): pl.pallas_call(functools.partial(layer, peer_count, slots, reduce_here),...  31 us
    pallas_call x1, Pallas kernels, on_device(): pl.pallas_call(functools.partial(spread_inputs, peer_count, slots), out_s...  14.4 us
    pallas_call x1, Pallas kernels, on_device(): pl.pallas_call(functools.partial(build_adjacency, dst_count, halo_blocks)...  9.32 us
    ppermute x1, starting transfers between devices, on_device(): grad_across = lax.ppermute(grad_out, 'rep', by_chip)  3 us
    pallas_call x1, Pallas kernels, on_device(): pl.pallas_call(deliver, out_shape=(shaped((quarter, width), jnp.bfloat16)...  2.57 us
  transfers between devices with their start and end apart: 3, of which 0 were waited for; matrix products, arithmetic and copies ran while one was open for 0% of the time, Pallas kernels for 38%

profile of v7, /device:TPU:0, one launch (start us, length us, event | category | flops | bytes accessed | tf_op | source)
XLA Modules:
  0.0 62.3 jit_solution(16884989962782044275)
XLA Ops:
  0.6 3.0 %collective-permute-start.1 = (bf16[256,512]{1,0:T(8,128)(2,1)}, bf16[256,512]{1,0:T(8,128)(2,1)S(1)}, u32[]{:S(2)}, u32[]{:S(2)}) collective-permute-start(bf16[256,512]{1,0:T(8,128)(2,1)} %grad_own.1), channel_id=1, source_target_pairs={{0,2},{1,3},{2,0},{3,1},{4,6},{5,7},{6,4},{7,5},{8,10},{9,11},{10,... | collective-permute-start | bytes 786440 | tf_op jit(solution)/shard_map/ppermute | solution.py:536
  3.6 0.0 collective-permute-start
  3.6 14.4 %spread_inputs.1 = (s32[4,256,128]{2,1,0:T(8,128)}, s32[4,16,128]{2,1,0:T(8,128)}, bf16[4,8,16,256]{3,2,1,0:T(8,128)(2,1)}) custom-call(s32[256,128]{1,0:T(8,128)} %bitcast.5, s32[1,128]{1,0:T(1,128)} %bitcast.8, s32[1,128]{1,0:T(1,128)} %bitcast.9, s32[8,8]{1,0:T(8,128)} %bitcast.6, bf16[1024,512]{1,0:T(8,128)(2,1)} %feats.3), custom_call_target="tpu_custom_call" | custom-call | tf_op jit(solution)/shard_map/spread_inputs/pallas_call | solution.py:543
  18.1 0.0 collective-permute-done.1.grad_across
  18.1 0.0 copy-start
  18.1 0.4 collective-permute-start.2
  18.5 9.3 %build_adjacency.1.adjacency_from = bf16[1024,1280]{1,0:T(8,128)(2,1)} custom-call(s32[4,16,128]{2,1,0:T(8,128)} %get-tuple-element.10.meta, s32[4,256,128]{2,1,0:T(8,128)} %get-tuple-element.11.bits), custom_call_target="tpu_custom_call" | custom-call | flops 8000000000 | bytes 4000000 | tf_op jit(solution)/shard_map/build_adjacency/pallas_call | solution.py:571
  27.9 0.0 copy-done
  27.9 0.0 collective-permute-done.grad_core
  27.9 0.0 copy-start.1
  27.9 0.0 collective-permute-done.2.grad_diagonal
  27.9 0.0 copy-start.2
  27.9 0.7 %copy-done.1 = bf16[256,512]{1,0:T(8,128)(2,1)} copy-done((bf16[256,512]{1,0:T(8,128)(2,1)}, bf16[256,512]{1,0:T(8,128)(2,1)S(1)}, u32[]{:S(2)}) %copy-start.1) | copy-done | bytes 262168
  28.6 0.1 copy-done.2
  28.7 31.0 %layer.1 = (bf16[256,512]{1,0:T(8,128)(2,1)}, bf16[256,512]{1,0:T(8,128)(2,1)}, bf16[2,512,512]{2,1,0:T(8,128)(2,1)}, bf16[256,512]{1,0:T(8,128)(2,1)}) custom-call(bf16[1024,1280]{1,0:T(8,128)(2,1)} %build_adjacency.1.adjacency_from, bf16[4,8,16,256]{3,2,1,0:T(8,128)(2,1)} %get-tuple-element.12.halo, s32[4,16,128]{2,1,0:T(8,128)} %get-tuple-element.10.meta, ...), custom_call_target="tpu_custom_call" | custom-call | tf_op jit(solution)/shard_map/layer/pallas_call | solution.py:593
  59.7 2.6 %deliver.1 = (bf16[256,512]{1,0:T(8,128)(2,1)}, bf16[256,512]{1,0:T(8,128)(2,1)}, bf16[512,512]{1,0:T(8,128)(2,1)}, bf16[512,512]{1,0:T(8,128)(2,1)}) custom-call(bf16[256,512]{1,0:T(8,128)(2,1)} %get-tuple-element.13.out_feats, bf16[256,512]{1,0:T(8,128)(2,1)} %get-tuple-element.14.grad_feats, bf16[2,512,512]{2,1,0:T(8,128)(2,1)} %get-tuple-element.15.weights), custom_call_target="tpu_custom_call" | custom-call | tf_op jit(solution)/shard_map/deliver/pallas_call | solution.py:639
Async XLA Ops:
  0.6 17.5 %collective-permute-start.1 = (bf16[256,512]{1,0:T(8,128)(2,1)}, bf16[256,512]{1,0:T(8,128)(2,1)S(1)}, u32[]{:S(2)}, u32[]{:S(2)}) collective-permute-start(bf16[256,512]{1,0:T(8,128)(2,1)} %grad_own.1), channel_id=1, source_target_pairs={{0,2},{1,3},{2,0},{3,1},{4,6},{5,7},{6,4},{7,5},{8,10},{9,11},{10,... | collective-permute-start | bytes 786440 | tf_op jit(solution)/shard_map/ppermute | solution.py:536
  3.6 24.2 %collective-permute-start = (bf16[256,512]{1,0:T(8,128)(2,1)}, bf16[256,512]{1,0:T(8,128)(2,1)S(1)}, u32[]{:S(2)}, u32[]{:S(2)}) collective-permute-start(bf16[256,512]{1,0:T(8,128)(2,1)} %grad_own.1), channel_id=1, source_target_pairs={{0,1},{1,0},{2,3},{3,2},{4,5},{5,4},{6,7},{7,6},{8,9},{9,8},{10,11... | collective-permute-start | bytes 786440 | tf_op jit(solution)/shard_map/ppermute | solution.py:537
  18.1 9.8 %copy-start = (bf16[256,512]{1,0:T(8,128)(2,1)}, bf16[256,512]{1,0:T(8,128)(2,1)S(1)}, u32[]{:S(2)}) copy-start(bf16[256,512]{1,0:T(8,128)(2,1)S(1)} %collective-permute-done.1.grad_across) | copy-start | bytes 786436
  18.1 9.8 %collective-permute-start.2 = (bf16[256,512]{1,0:T(8,128)(2,1)S(1)}, bf16[256,512]{1,0:T(8,128)(2,1)S(1)}, u32[]{:S(2)}, u32[]{:S(2)}) collective-permute-start(bf16[256,512]{1,0:T(8,128)(2,1)S(1)} %collective-permute-done.1.grad_across), channel_id=1, source_target_pairs={{0,1},{1,0},{2,3},{3,2},{4,5},{5,4},{6,7},{7,6},{8,9},{9,8},{10,11... | collective-permute-start | bytes 786440 | tf_op jit(solution)/shard_map/ppermute | solution.py:538
  27.9 0.7 %copy-start.1 = (bf16[256,512]{1,0:T(8,128)(2,1)}, bf16[256,512]{1,0:T(8,128)(2,1)S(1)}, u32[]{:S(2)}) copy-start(bf16[256,512]{1,0:T(8,128)(2,1)S(1)} %collective-permute-done.grad_core) | copy-start | bytes 786436
  27.9 0.8 %copy-start.2 = (bf16[256,512]{1,0:T(8,128)(2,1)}, bf16[256,512]{1,0:T(8,128)(2,1)S(1)}, u32[]{:S(2)}) copy-start(bf16[256,512]{1,0:T(8,128)(2,1)S(1)} %collective-permute-done.2.grad_diagonal) | copy-start | bytes 786436
